TPU v7x, 32 devices: a whole 2x2x4 slice. The times are simulated.
32 devices in a mesh: groups: 2 (over y), req: 4 (over z), tp: 4 (over x, core).
Axes of the slice: x: 2, y: 2, z: 4, core: 2. Of those that a mesh axis runs over, the one named last changes fastest.
Arguments:
- patches: bfloat16 [512, 1280], P(('groups', 'req'), 'tp'), parts along dimension 0, may hold values from -6 to 6
- patch_counts: int32 [8, 2], P('groups'), parts along dimension 0, may hold values from 4 to 32, as said below
- image_request: int32 [8, 2], P('groups'), parts along dimension 0, may hold values from 0 to 3, as said below
- image_position: int32 [8, 2], P('groups'), parts along dimension 0, may hold values from 0 to 504, as said below
- request_lengths: int32 [8], P('groups'), parts along dimension 0, may hold values from 1 to 512, as said below
- vit_gain: float32 [1280], replicated, may hold values from 0.1 to 1.9
- qkv_weight: bfloat16 [1280, 3, 1280], P('req', None, 'tp'), may hold values from -2 to 2
- proj_weight: bfloat16 [1280, 1280], P('tp', 'req'), may hold values from -0.15625 to 0.15625
- merge_gain: float32 [1280], replicated, may hold values from 0.1 to 1.9
- fc1_weight: bfloat16 [5120, 5120], P('req', 'tp'), may hold values from -0.078125 to 0.078125
- fc2_weight: bfloat16 [5120, 8192], P('tp', 'req'), may hold values from -0.078125 to 0.078125
- text_rows: bfloat16 [4096, 8192], P(('groups', 'req'), 'tp'), parts along dimension 0, may hold values from -6 to 6
- rms_gain: float32 [8192], P('tp'), may hold values from 0.1 to 1.9
- kv_weight: bfloat16 [8192, 2, 1024], P('tp'), may hold values from -0.0625 to 0.0625
- kv_scale: float32 [2, 16], replicated, may hold values from 0.004 to 0.04
Outputs:
- kv_cache: bfloat16 [4096, 2, 1024], P(('groups', 'req', 'tp')), parts along dimension 0
There are 2 independent parts, one for each index of `groups`. A program takes and returns all parts, laid end to end along the dimension named above; an argument that names none is the same for every part. Nothing has to cross between parts.
Inputs may be any that keep to these rules, and one draw needn't show every extreme that they name: `patch_counts`: multiples of 4. The images of block s are those of row s; the largest count is reached in every draw. `image_request`: every block of 512 rows of combined holds the placeholders of exactly 2 whole images, at most 16 placeholder rows, and some block holds exactly 16. `image_position`: placeholders of different images never share a row and never cross a block of 512 rows. `request_lengths`: every placeholder row lies before its request's length; one request fills its whole slot.
All inputs are finite; a program needn't handle non-finite values.
Results may differ from a plain program's by a relative error of at most 0.0052.
Values may be sent and summed in bfloat16 or wider, within the bound.
A program may use at most 128 MiB of HBM per device.

v0:
```python
import jax
import jax.numpy as jnp
from jax import lax
from jax.sharding import PartitionSpec as P

VIT_HEADS = 16
VIT_HD = 80
D = 8192
KV_HEADS = 8
HEAD_DIM = 128
QGROUP = 64


epsilon = 1e-06
theta_base = 1000000.0
clip_level = 127.0


def layer_norm(values, gains):
    average = jnp.mean(values, axis=-1, keepdims=True)
    centred = values - average
    variance = jnp.mean(centred * centred, axis=-1, keepdims=True)
    return centred * lax.rsqrt(variance + epsilon) * gains


def patch_images(counts_row, patch_rows):
    bounds = jnp.cumsum(counts_row)
    row_ids = jnp.arange(patch_rows, dtype=jnp.int32)
    return jnp.sum((row_ids[:, None] >= bounds[None, :]).astype(jnp.int32), axis=1)


def attend(queries, keys_in, values_in, image_ids, factor):
    scores = (
        jnp.einsum("qhd,khd->hqk", queries, keys_in, preferred_element_type=jnp.float32) * factor
    )
    allowed = image_ids[:, None] == image_ids[None, :]
    scores = jnp.where(allowed[None], scores, -jnp.inf)
    weights = jax.nn.softmax(scores, axis=-1).astype(jnp.bfloat16)
    return jnp.einsum(
        "hqk,khd->qhd", weights, values_in, preferred_element_type=jnp.float32
    ).astype(jnp.bfloat16)


def visual_targets(patch_counts, image_request, image_position, merged_dev, request_len):
    merged_runs = patch_counts // 4
    run_ends = jnp.cumsum(merged_runs, axis=1)
    run_starts = run_ends - merged_runs
    row_ids = jnp.arange(merged_dev, dtype=jnp.int32)
    inside = (row_ids[None, :, None] >= run_starts[:, None, :]) & (
        row_ids[None, :, None] < run_ends[:, None, :]
    )
    offsets = image_request * request_len + image_position - run_starts
    target = jnp.sum(jnp.where(inside, offsets[:, None, :] + row_ids[None, :, None], 0), axis=2)
    is_live = jnp.any(inside, axis=2)
    return (target.reshape(-1), is_live.reshape(-1))


def rotate_keys(heads, positions):
    half_dim = heads.shape[-1] // 2
    frequency = theta_base ** (-2.0 * jnp.arange(half_dim, dtype=jnp.float32) / heads.shape[-1])
    angles = positions.astype(jnp.float32)[:, None] * frequency[None, :]
    cosine = jnp.cos(angles)[:, None, :]
    sine = jnp.sin(angles)[:, None, :]
    former = heads[..., :half_dim]
    latter = heads[..., half_dim:]
    return jnp.concatenate(
        [former * cosine - latter * sine, latter * cosine + former * sine], axis=-1
    )


def finish_cache(stacked, positions, live_rows, kv_scale):
    height = stacked.shape[0]
    rotated = rotate_keys(stacked[:, 0].reshape(height, KV_HEADS, HEAD_DIM), positions)
    joined = jnp.concatenate(
        [rotated.reshape(height, 1, KV_HEADS * HEAD_DIM), stacked[:, 1:2]], axis=1
    )
    bounds = jnp.repeat(clip_level * kv_scale, QGROUP, axis=1)
    clipped = jnp.clip(joined, -bounds, bounds)
    return jnp.where(live_rows[:, None, None], clipped, 0.0).astype(jnp.bfloat16)


def body(
    patches,
    patch_counts,
    image_request,
    image_position,
    request_lengths,
    vit_gain,
    qkv_weight,
    proj_weight,
    merge_gain,
    fc1_weight,
    fc2_weight,
    text_rows,
    rms_gain,
    kv_weight,
    kv_scale,
):
    req_devices = lax.axis_size("req")
    tp_devices = lax.axis_size("tp")
    req_index = lax.axis_index("req")
    tp_index = lax.axis_index("tp")
    patch_rows = patches.shape[0]
    merged_rows = patch_rows // 4
    token_rows = text_rows.shape[0]
    request_len = req_devices * token_rows // request_lengths.shape[0]
    local_heads = VIT_HEADS // tp_devices
    gathered = lax.all_gather(patches, "tp", axis=1, tiled=True)
    vit_width = gathered.shape[1]
    normed = layer_norm(gathered.astype(jnp.float32), vit_gain).astype(jnp.bfloat16)
    qkv_local = jnp.einsum(
        "pd,dcf->pcf",
        normed,
        lax.all_gather(qkv_weight, "req", axis=0, tiled=True),
        preferred_element_type=jnp.float32,
    ).astype(jnp.bfloat16)
    heads = qkv_local.reshape(patch_rows, 3, local_heads, VIT_HD)
    image_ids = patch_images(patch_counts[req_index], patch_rows)
    attended = attend(heads[:, 0], heads[:, 1], heads[:, 2], image_ids, VIT_HD ** (-0.5))
    flat_heads = attended.reshape(patch_rows, local_heads * VIT_HD)
    branch = jnp.dot(
        flat_heads,
        lax.all_gather(proj_weight, "req", axis=1, tiled=True),
        preferred_element_type=jnp.float32,
    )
    branch_total = lax.psum(branch, "tp")
    hidden = (gathered.astype(jnp.float32) + branch_total).astype(jnp.bfloat16)
    merged_norm = layer_norm(hidden.astype(jnp.float32), merge_gain).astype(jnp.bfloat16)
    merged = merged_norm.reshape(merged_rows, 4 * vit_width)
    feature_blocks = lax.all_to_all(merged, "req", split_axis=1, concat_axis=0, tiled=True)
    picked = feature_blocks
    before_gelu = lax.psum_scatter(
        jnp.dot(picked, fc1_weight, preferred_element_type=jnp.float32),
        "req",
        scatter_dimension=0,
        tiled=True,
    )
    activated = jax.nn.gelu(before_gelu, approximate=False).astype(jnp.bfloat16)
    outward = jnp.dot(
        lax.all_gather(activated, "req", axis=0, tiled=True),
        fc2_weight,
        preferred_element_type=jnp.float32,
    )
    target, is_live = visual_targets(
        patch_counts, image_request, image_position, merged_rows, request_len
    )
    all_rows = req_devices * token_rows
    slot_total = req_devices * merged_rows
    source_total = outward.shape[0]
    flags = (
        jnp.zeros((all_rows,), jnp.int32)
        .at[jnp.where(is_live, target, all_rows)]
        .set(1, mode="drop")
    )
    flag_grid = flags.reshape(req_devices, token_rows)
    ranks = (jnp.cumsum(flag_grid, axis=1) - flag_grid).reshape(-1)
    owners = target // token_rows
    slots = owners * merged_rows + ranks[jnp.clip(target, 0, all_rows - 1)]
    source_ids = jnp.arange(source_total, dtype=jnp.int32)
    picking = (
        jnp.full((slot_total,), source_total, jnp.int32)
        .at[jnp.where(is_live, slots, slot_total)]
        .set(source_ids, mode="drop")
    )
    padded = jnp.concatenate([outward, jnp.zeros((1, outward.shape[1]), jnp.float32)], axis=0)
    sending = padded[picking]
    arrived = lax.all_to_all(sending, "req", split_axis=0, concat_axis=1, tiled=True)
    visual = lax.psum_scatter(arrived, "tp", scatter_dimension=1, tiled=True).astype(jnp.bfloat16)
    local_flags = lax.dynamic_slice_in_dim(flags, req_index * token_rows, token_rows)
    local_ranks = lax.dynamic_slice_in_dim(ranks, req_index * token_rows, token_rows)
    chosen = visual[jnp.clip(local_ranks, 0, merged_rows - 1)]
    combined = jnp.where(local_flags[:, None] > 0, chosen, text_rows)
    wide_rows = combined.astype(jnp.float32)
    square_sums = lax.psum(jnp.sum(wide_rows * wide_rows, axis=1), "tp")
    scaled = (wide_rows * lax.rsqrt(square_sums[:, None] / D + epsilon) * rms_gain).astype(
        jnp.bfloat16
    )
    share_rows = token_rows // tp_devices
    picked = scaled
    stacked = lax.psum_scatter(
        jnp.einsum("rf,fcw->rcw", picked, kv_weight, preferred_element_type=jnp.float32),
        "tp",
        scatter_dimension=0,
        tiled=True,
    )
    row_ids = (
        req_index * token_rows + tp_index * share_rows + jnp.arange(share_rows, dtype=jnp.int32)
    )
    positions = row_ids % request_len
    live_rows = positions < request_lengths[row_ids // request_len]
    return finish_cache(stacked, positions, live_rows, kv_scale)


def solution(mesh):
    placed = (
        P(("groups", "req"), "tp"),
        P("groups", None),
        P("groups", None),
        P("groups", None),
        P("groups"),
        P(),
        P("req", None, "tp"),
        P("tp", "req"),
        P(),
        P("req", "tp"),
        P("tp", "req"),
        P(("groups", "req"), "tp"),
        P("tp"),
        P("tp", None, None),
        P(),
    )
    return jax.shard_map(
        body,
        mesh=mesh,
        in_specs=placed,
        out_specs=P(("groups", "req", "tp"), None, None),
        check_vma=False,
    )
```

profile of v0, /device:TPU:1, one launch (start us, length us, event | category | flops | bytes accessed | tf_op | source)
XLA Modules:
  0.0 302.1 jit_solution(17117356002991101035)
XLA Ops:
  6.5 0.7 all-gather.3.cloned.1.call-update
  7.3 7.1 %all-gather = bf16[4,320,64]{1,2,0:T(8,128)(2,1)S(1)} all-gather(bf16[1,320,64]{1,2,0:T(8,128)(2,1)} %bitcast.89), channel_id=1, replica_groups=mesh['groups'=2,'req'=4,'tp'=4] {'tp'}, dimensions={0}, use_global_device_ids=true | all-gather | bytes 204800 | tf_op jit(solution)/shard_map/all_gather | solution.py:108
  14.4 0.9 copy.54
  15.3 2.0 reshape.503
  17.3 0.9 dynamic-slice_reduce_fusion
  18.3 1.8 copy.60
  20.1 0.7 and_select_fusion.1
  20.9 0.7 add_subtract_fusion
  23.2 1.2 multiply_reduce_fusion
  24.5 37.6 %all_gather.14 = bf16[320,1280]{0,1:T(8,128)(2,1)} all-gather(bf16[320,320]{0,1:T(8,128)(2,1)} %copy.60), channel_id=1, replica_groups=mesh['groups'=2,'req'=4,'tp'=4] {'req'}, dimensions={1}, use_global_device_ids=true | all-gather | bytes 1024000 | tf_op jit(solution)/shard_map/all_gather | solution.py:123
  62.1 24.8 %all-gather.3.cloned.1.call-done = bf16[1280,3,320]{2,0,1:T(8,128)(2,1)} async-done(((bf16[320,3,320]{2,0,1:T(8,128)(2,1)}), bf16[1280,3,320]{2,0,1:T(8,128)(2,1)}) %all-gather.3.cloned.1.call-update) | async-done | bytes 2457616 | tf_op jit(solution)/shard_map/all_gather | solution.py:114
  86.9 3.3 %convolution_convert_fusion = bf16[64,3,320]{2,0,1:T(8,128)(2,1)} fusion(bf16[1280,3,320]{2,0,1:T(8,128)(2,1)} %all-gather.3.cloned.1.call-done, f32[1280,64]{0,1:T(8,128)} %reshape.503, f32[1280]{0:T(1024)S(1)} %copy-done.1, f32[64]{0:T(128)S(1)} %add_rsqrt_fusion.2, f32[64]{0:T(128)S(1)} %broadcast_multiply_fusion.2), kind=kOutput, calls=%fused_computation.17 | convolution fusion | flops 157675520 | bytes 2913792 | tf_op jit(solution)/shard_map/pd,dcf->pcf/dot_general | solution.py:111
  90.1 1.1 reshape.426
  92.1 1.2 fusion.13
  93.5 2.4 fusion.59
  95.9 0.7 fusion.47
  96.6 0.8 scatter_custom_fusion
  97.3 1.2 reduce-window.19
  98.6 27.0 %all-reduce.3.cloned.1.call-done = f32[64,1280]{1,0:T(8,128)} async-done(((f32[64,1280]{1,0:T(8,128)}), f32[64,1280]{1,0:T(8,128)}) %all-reduce.3.cloned.1.call-update) | async-done | bytes 327696 | tf_op jit(solution)/shard_map/psum | solution.py:126
  125.6 1.2 convert_reduce_fusion
  127.1 0.7 all_to_all.28
  127.9 1.6 copy.61
  129.4 4.8 %all-to-all-start = ((bf16[16,4,1280]{2,0,1:T(8,128)(2,1)}), bf16[16,4,1280]{2,0,1:T(8,128)(2,1)S(1)}, u32[]{:S(2)}, u32[]{:S(2)}) async-start(bf16[16,4,1280]{2,0,1:T(8,128)(2,1)} %copy.61), calls=%async_computation | async-start | bytes 327680 | tf_op jit(solution)/shard_map/all_to_all | solution.py:130
  134.7 4.4 %all-to-all-done = bf16[16,4,1280]{2,0,1:T(8,128)(2,1)S(1)} async-done(((bf16[16,4,1280]{2,0,1:T(8,128)(2,1)}), bf16[16,4,1280]{2,0,1:T(8,128)(2,1)S(1)}, u32[]{:S(2)}, u32[]{:S(2)}) %all-to-all-start) | async-done | bytes 163872 | tf_op jit(solution)/shard_map/all_to_all | solution.py:130
  139.1 1.4 fusion.60
  140.6 0.8 gather_fusion
  141.4 0.8 scatter_custom_fusion.1
  142.2 17.9 %reduce-scatter.4.cloned.1.call-done = f32[16,1280]{1,0:T(8,128)} async-done(((f32[64,1280]{1,0:T(8,128)}), f32[16,1280]{1,0:T(8,128)}) %reduce-scatter.4.cloned.1.call-update) | async-done | bytes 81936 | tf_op jit(solution)/shard_map/reduce_scatter | solution.py:132
  160.1 1.1 fusion.30
  161.2 10.7 %all_gather.15 = bf16[64,1280]{1,0:T(8,128)(2,1)S(1)} all-gather(bf16[16,1280]{1,0:T(8,128)(2,1)S(1)} %fusion.30), channel_id=1, replica_groups=mesh['groups'=2,'req'=4,'tp'=4] {'req'}, dimensions={0}, use_global_device_ids=true | all-gather | bytes 204800 | tf_op jit(solution)/shard_map/all_gather | solution.py:140
  171.8 3.5 %fusion.61 = f32[64,2048]{1,0:T(8,128)S(1)} fusion(bf16[64,1280]{1,0:T(8,128)(2,1)S(1)} %all_gather.15, bf16[1280,2048]{1,0:T(8,128)(2,1)} %param.25), kind=kOutput, calls=%fused_computation.141 | convolution fusion | flops 335544320 | bytes 5931008 | tf_op jit(solution)/shard_map/dot_general | solution.py:139
  175.4 0.9 concatenate.9
  176.2 2.8 gather_fusion.1
  179.1 12.7 %all_to_all.38 = f32[4,16,2048]{2,1,0:T(8,128)S(1)} all-to-all(f32[4,16,2048]{2,1,0:T(8,128)} %bitcast.84), channel_id=1, replica_groups=mesh['groups'=2,'req'=4,'tp'=4] {'req'}, dimensions={0} | all-to-all | bytes 1048576 | tf_op jit(solution)/shard_map/all_to_all | solution.py:167
  191.7 0.8 copy.69
  192.8 26.2 %reduce-scatter.6.cloned.1.call-done = f32[16,2048]{1,0:T(8,128)} async-done(((f32[16,8192]{1,0:T(8,128)}), f32[16,2048]{1,0:T(8,128)}) %reduce-scatter.6.cloned.1.call-update) | async-done | bytes 131088 | tf_op jit(solution)/shard_map/reduce_scatter | solution.py:168
  219.0 0.9 convert_element_type.64
  219.9 3.3 %gather_fusion.2 = bf16[512,2048]{1,0:T(8,128)(2,1)} fusion(bf16[16,2048]{1,0:T(8,128)(2,1)S(1)} %convert_element_type.64, s32[1024]{0:T(1024)S(1)} %pad_clamp_fusion), kind=kCustom, calls=%fused_computation.2 | custom fusion | bytes 4196352 | tf_op jit(solution)/shard_map/gather | solution.py:171
  223.2 3.1 %fusion.3 = f32[512]{0:T(512)S(1)} fusion(bf16[512,2048]{1,0:T(8,128)(2,1)} %gather_fusion.2, bf16[512,2048]{1,0:T(8,128)(2,1)} %param.26, pred[512]{0:T(512)(128)(4,1)S(1)} %dynamic-slice_compare_fusion), kind=kLoop, calls=%fused_computation.10 | loop fusion | flops 4193792 | bytes 4196864 | tf_op jit(solution)/shard_map/reduce_sum | solution.py:174
  226.3 5.9 %psum.15 = f32[512]{0:T(512)S(1)} all-reduce(f32[512]{0:T(512)S(1)} %fusion.3), channel_id=1, replica_groups=mesh['groups'=2,'req'=4,'tp'=4] {'tp'}, use_global_device_ids=true, to_apply=%region_19.20 | all-reduce | flops 512 | bytes 4096 | tf_op jit(solution)/shard_map/psum | solution.py:174
  232.1 11.5 %fusion.1 = f32[512,2,1024]{2,0,1:T(8,128)} fusion(bf16[2048,2,1024]{2,1,0:T(2,128)(2,1)} %param.28, f32[2048]{0:T(1024)S(1)} %copy-done.7, f32[512]{0:T(512)S(1)} %add_rsqrt_fusion, bf16[512,2048]{1,0:T(8,128)(2,1)} %gather_fusion.2, bf16[512,2048]{1,0:T(8,128)(2,1)} %param.26, pred[512]{0:T(512)(128)(4,1)S(1)} %dynamic-slice_compare_fusion), kind=kOutput, calls=%fused_computation.6 | convolution fusion | flops 4300210176 | bytes 16787968 | tf_op jit(solution)/shard_map/rf,fcw->rcw/dot_general | solution.py:181
  245.3 2.6 fusion.44
  248.2 41.3 %reduce-scatter.8.cloned.1.call-done = f32[128,2,1024]{2,0,1:T(8,128)} async-done(((f32[512,2,1024]{2,0,1:T(8,128)}), f32[128,2,1024]{2,0,1:T(8,128)}) %reduce-scatter.8.cloned.1.call-update) | async-done | bytes 1048592 | tf_op jit(solution)/shard_map/reduce_scatter | solution.py:180
  289.5 1.1 slice_bitcast_fusion
  291.1 0.8 reshape.432
  291.9 1.1 slice.54
  293.0 1.2 fusion.16
  294.2 1.3 copy.64
  (72 shorter events, 6.5 us)
Async XLA Ops:
  6.5 132.6 %copy-start = (bf16[1280,1280]{1,0:T(8,128)(2,1)S(1)}, bf16[1280,1280]{1,0:T(8,128)(2,1)}, u32[]{:S(2)}) copy-start(bf16[1280,1280]{1,0:T(8,128)(2,1)} %param.24) | copy-start | bytes 9830404
  6.5 80.3 %copy-start.1 = (f32[1280]{0:T(1024)S(1)}, f32[1280]{0:T(1024)}, u32[]{:S(2)}) copy-start(f32[1280]{0:T(1024)} %param.20) | copy-start | bytes 15364
  6.5 80.3 %all-gather.3.cloned.1.call-start = ((), (), s32[]{:S(2)}) async-start(), calls=%async_computation.5 | async-start | bytes 3686400 | tf_op jit(solution)/shard_map/all_gather | solution.py:114
  7.3 118.3 %all-reduce.3.cloned.1.call-start = ((), (), s32[]{:S(2)}) async-start(), calls=%async_computation.6 | async-start | bytes 655360 | tf_op jit(solution)/shard_map/psum | solution.py:126
  62.1 64.9 %copy-start.3 = (f32[1280]{0:T(1024)S(1)}, f32[1280]{0:T(1024)}, u32[]{:S(2)}) copy-start(f32[1280]{0:T(1024)} %param.23) | copy-start | bytes 15364
  91.5 0.7 copy-start.8
  126.8 14.6 %copy-start.4 = (s32[64,1]{0,1:T(1,128)S(1)}, s32[64,1]{0,1:T(1,128)}, u32[]{:S(2)}) copy-start(s32[64,1]{0,1:T(1,128)} %reshape.425) | copy-start | bytes 772
  126.8 14.6 %copy-start.5 = (pred[64,1]{0,1:T(4,128)(4,1)S(1)}, pred[64,1]{0,1:T(4,128)(4,1)}, u32[]{:S(2)}) copy-start(pred[64,1]{0,1:T(4,128)(4,1)} %reshape.424) | copy-start | bytes 196
  129.4 9.7 %all-to-all-start = ((bf16[16,4,1280]{2,0,1:T(8,128)(2,1)}), bf16[16,4,1280]{2,0,1:T(8,128)(2,1)S(1)}, u32[]{:S(2)}, u32[]{:S(2)}) async-start(bf16[16,4,1280]{2,0,1:T(8,128)(2,1)} %copy.61), calls=%async_computation | async-start | bytes 327680 | tf_op jit(solution)/shard_map/all_to_all | solution.py:130
  134.2 25.8 %reduce-scatter.4.cloned.1.call-start = ((), (), s32[]{:S(2)}) async-start(), calls=%async_computation.7 | async-start | bytes 409600 | tf_op jit(solution)/shard_map/reduce_scatter | solution.py:132
  140.6 78.4 %reduce-scatter.6.cloned.1.call-start = ((), (), s32[]{:S(2)}) async-start(), calls=%async_computation.8 | async-start | bytes 655360 | tf_op jit(solution)/shard_map/reduce_scatter | solution.py:168
  192.6 96.9 %reduce-scatter.8.cloned.1.call-start = ((), (), s32[]{:S(2)}) async-start(), calls=%async_computation.9 | async-start | bytes 5242880 | tf_op jit(solution)/shard_map/reduce_scatter | solution.py:180
  223.2 8.9 %copy-start.7 = (f32[2048]{0:T(1024)S(1)}, f32[2048]{0:T(1024)}, u32[]{:S(2)}) copy-start(f32[2048]{0:T(1024)} %param.27) | copy-start | bytes 24580
  243.7 0.7 copy-start.6
  243.7 0.9 copy-start.2
Sparse Core Ops, SparseCore 0:
  8.9 77.8 all-gather.2
  96.0 29.5 all-reduce.2
  140.7 19.3 reduce-scatter.3
  192.7 26.2 reduce-scatter.5
  243.8 45.6 reduce-scatter.7
where the time goes:
time: 304 us; the launch traced here: 302 us
  waiting for transfers between devices  142 us (47%)
  blocking collectives  73.8 us (24%)
  local copies, waits for them, and re-layouts  27.3 us (9%)
  matrix products  23.5 us (8%)
  other arithmetic  16.8 us (6%)
  between operations  13.4 us (4%)
  starting transfers between devices  4.92 us (2%)
    reduce_scatter x1, waiting for transfers between devices, body(): lax.psum_scatter(jnp.einsum('rf,fcw->rcw', picked, kv_weight, preferred_e...  41.3 us
    all_gather x1, blocking collectives, body(): lax.all_gather(proj_weight, 'req', axis=1, tiled=True)  37.6 us
    psum x1, waiting for transfers between devices, body(): branch_total = lax.psum(branch, 'tp')  27 us
    reduce_scatter x1, waiting for transfers between devices, body(): lax.psum_scatter(arrived, 'tp', scatter_dimension=1, tiled=True)  26.2 us
    all_gather x1, waiting for transfers between devices, body(): lax.all_gather(qkv_weight, 'req', axis=0, tiled=True)  24.8 us
    reduce_scatter x1, waiting for transfers between devices, body(): lax.psum_scatter(jnp.dot(picked, fc1_weight, preferred_element_type=jnp.f...  17.9 us
    all_to_all x1, blocking collectives, body(): lax.all_to_all(sending, 'req', split_axis=0, concat_axis=1, tiled=True)  12.7 us
    dot_general x1, matrix products, body(): jnp.einsum('rf,fcw->rcw', picked, kv_weight, preferred_element_type=jnp.f...  11.5 us
  transfers between devices with their start and end apart: 6, of which 6 were waited for; matrix products, arithmetic and copies ran while one was open for 6% of the time, Pallas kernels for 0%

commit v1 on v0

--- a/solution.py
+++ b/solution.py
@@ -1,6 +1,10 @@
+import functools
+
 import jax
 import jax.numpy as jnp
 from jax import lax
+from jax.experimental import pallas as pl
+from jax.experimental.pallas import tpu as pltpu
 from jax.sharding import PartitionSpec as P
 
 VIT_HEADS = 16
@@ -79,7 +83,7 @@
     return jnp.where(live_rows[:, None, None], clipped, 0.0).astype(jnp.bfloat16)
 
 
-def body(
+def general_body(
     patches,
     patch_counts,
     image_request,
@@ -191,6 +195,495 @@
     return finish_cache(stacked, positions, live_rows, kv_scale)
 
 
+def iota(shape, dim):
+    return lax.broadcasted_iota(jnp.int32, shape, dim)
+
+
+def f32_dot(left, right):
+    return jnp.dot(left, right, preferred_element_type=jnp.float32)
+
+
+def image_table(counts, image_request, image_position, request_len, token_rows):
+    images = []
+    for s in range(counts.shape[0]):
+        source = jnp.int32(s * SLOTS)
+        for j in range(counts.shape[1]):
+            run = counts[s, j] // 4
+            first = image_request[s, j] * request_len + image_position[s, j]
+            images.append((source, first, run, first // token_rows))
+            source = source + run
+    table = []
+    for source, first, run, owner in images:
+        base = jnp.int32(0)
+        for _, other_first, other_run, other_owner in images:
+            earlier = (other_owner == owner) & (other_first < first)
+            base = base + jnp.where(earlier, other_run, 0)
+        table.append((source, first, run, owner, base))
+    return table
+
+
+SLOTS = 16
+SIDE = 4
+
+
+def vision_kernel(
+    request_len,
+    token_rows,
+    counts,
+    image_request,
+    image_position,
+    patches,
+    vit_gain,
+    merge_gain,
+    rms_gain,
+    qkv_hbm,
+    proj_hbm,
+    fc1_hbm,
+    fc2_hbm,
+    kv_hbm,
+    placed_ref,
+    qkv_w,
+    proj_w,
+    fc1_w,
+    fc2_w,
+    kv_w,
+    load_sem,
+    patch_all,
+    res_out,
+    res_in,
+    norm_out,
+    norm_in,
+    part_own,
+    part_out,
+    part_in,
+    att_out,
+    att_in,
+    branch_out,
+    branch_in,
+    hid_out,
+    hid_in,
+    pre_own,
+    pre_out,
+    pre_in,
+    act_out,
+    act_in,
+    vis_out,
+    vis_in,
+    row_out,
+    row_in,
+    sq_out,
+    sq_in,
+    send_sem,
+    recv_sem,
+):
+    r = lax.axis_index("req")
+    t = lax.axis_index("tp")
+    rows, width = patches.shape
+    full = SIDE * width
+
+    def other(i, d):
+        return lax.rem(i + d, SIDE)
+
+    loads = []
+    for k, (src, dst) in enumerate(
+        ((qkv_hbm, qkv_w), (proj_hbm, proj_w), (fc1_hbm, fc1_w), (fc2_hbm, fc2_w), (kv_hbm, kv_w))
+    ):
+        copy = pltpu.make_async_copy(src, dst, load_sem.at[k])
+        copy.start()
+        loads.append(copy)
+
+    barrier = pltpu.get_barrier_semaphore()
+    for a in range(SIDE):
+        for b in range(SIDE):
+            if a or b:
+                pl.semaphore_signal(
+                    barrier,
+                    inc=1,
+                    device_id={"req": other(r, a), "tp": other(t, b)},
+                    device_id_type=pl.DeviceIdType.MESH,
+                )
+    pl.semaphore_wait(barrier, SIDE * SIDE - 1)
+
+    pending = []
+
+    def remote(src, dst, stage, s_index, r_index, to_r, to_t):
+        return pltpu.make_async_remote_copy(
+            src_ref=src,
+            dst_ref=dst,
+            send_sem=send_sem.at[stage, s_index],
+            recv_sem=recv_sem.at[stage, r_index],
+            device_id={"req": to_r, "tp": to_t},
+            device_id_type=pl.DeviceIdType.MESH,
+        )
+
+    def send(copy, unless=None):
+        if unless is None:
+            copy.start()
+            pending.append(copy.wait_send)
+        else:
+            pl.when(jnp.logical_not(unless))(copy.start)
+            pending.append(lambda: pl.when(jnp.logical_not(unless))(copy.wait_send))
+
+    def receive(dst, stage, index, unless=None):
+        copy = remote(dst, dst, stage, 0, index, other(r, 1), t)
+        if unless is None:
+            copy.wait_recv()
+        else:
+            pl.when(jnp.logical_not(unless))(copy.wait_recv)
+
+    on_diagonal = r == t
+
+    for d in range(1, SIDE):
+        send(remote(patches, patch_all.at[t], 0, d, d, r, other(t, d)))
+    patch_all[t] = patches[...]
+    picks_i = iota((rows, rows), 0)
+    picks_j = iota((rows, rows), 1)
+    by_class = jnp.where(
+        picks_j == 4 * lax.rem(picks_i, SLOTS) + picks_i // SLOTS, 1.0, 0.0
+    ).astype(jnp.bfloat16)
+    regrouped = f32_dot(by_class, patches[...]).astype(jnp.bfloat16)
+    for c in range(SIDE):
+        res_out[c] = regrouped[c * SLOTS : (c + 1) * SLOTS]
+    for d in range(SIDE):
+        c = other(t, d)
+        unless = on_diagonal if d == 0 else None
+        send(remote(res_out.at[c], res_in.at[r], 1, d, r, t, c), unless)
+
+    @pl.when(on_diagonal)
+    def _():
+        res_in[r] = res_out[t]
+
+    for d in range(1, SIDE):
+        receive(patch_all.at[other(t, SIDE - d)], 0, d)
+
+    def chunk_norm(values, gains):
+        total = jnp.sum(values[0], axis=1, keepdims=True)
+        for v in values[1:]:
+            total = total + jnp.sum(v, axis=1, keepdims=True)
+        average = total / full
+        centred = [v - average for v in values]
+        total = jnp.sum(centred[0] * centred[0], axis=1, keepdims=True)
+        for v in centred[1:]:
+            total = total + jnp.sum(v * v, axis=1, keepdims=True)
+        inverse = lax.rsqrt(total / full + epsilon)
+        return [
+            (v * inverse * gains[c : c + 1, :]).astype(jnp.bfloat16)
+            for c, v in enumerate(centred)
+        ]
+
+    normed = chunk_norm([patch_all[c].astype(jnp.float32) for c in range(SIDE)], vit_gain)
+    for c in range(SIDE):
+        norm_out[c] = normed[c]
+    for d in range(1, SIDE):
+        p = other(r, d)
+        send(remote(norm_out.at[p], norm_in.at[r], 2, d, d, p, t))
+    norm_in[r] = norm_out[r]
+    for d in range(1, SIDE):
+        receive(norm_in.at[other(r, SIDE - d)], 2, d)
+
+    loads[0].wait()
+    every = norm_in[...].reshape(SIDE * rows, width)
+    for c in range(3):
+        part = f32_dot(every, qkv_w[c]).reshape(SIDE, rows, width)
+        part_own[:, c] = part
+        part_out[:, c] = part.astype(jnp.bfloat16)
+    for d in range(1, SIDE):
+        p = other(r, d)
+        send(remote(part_out.at[p], part_in.at[d - 1], 3, d, d, p, t))
+    total = part_own[r]
+    for d in range(1, SIDE):
+        receive(part_in.at[d - 1], 3, d)
+        total = total + part_in[d - 1].astype(jnp.float32)
+    qkv = total.astype(jnp.bfloat16)
+
+    first_end = counts[r, 0]
+    second_end = first_end + counts[r, 1]
+
+    def ids(index):
+        return (index >= first_end).astype(jnp.int32) + (index >= second_end).astype(jnp.int32)
+
+    allowed = ids(picks_i) == ids(picks_j)
+    lanes = iota((rows, width), 1) // VIT_HD
+    attended = jnp.zeros((rows, width), jnp.float32)
+    for h in range(width // VIT_HD):
+        mine = lanes == h
+        query = jnp.where(mine, qkv[0].astype(jnp.float32), 0.0).astype(jnp.bfloat16)
+        value = jnp.where(mine, qkv[2].astype(jnp.float32), 0.0).astype(jnp.bfloat16)
+        scores = lax.dot_general(
+            query, qkv[1], (((1,), (1,)), ((), ())), preferred_element_type=jnp.float32
+        ) * (VIT_HD ** (-0.5))
+        scores = jnp.where(allowed, scores, -jnp.inf)
+        weights = jnp.exp(scores - jnp.max(scores, axis=1, keepdims=True))
+        weights = weights / jnp.sum(weights, axis=1, keepdims=True)
+        attended = attended + f32_dot(weights.astype(jnp.bfloat16), value)
+    att_out[...] = f32_dot(by_class, attended.astype(jnp.bfloat16)).astype(jnp.bfloat16)
+    for d in range(1, SIDE):
+        send(remote(att_out, att_in.at[r], 4, d, d, other(r, d), t))
+    att_in[r] = att_out[...]
+    loads[1].wait()
+    for d in range(1, SIDE):
+        receive(att_in.at[other(r, SIDE - d)], 4, d)
+
+    branch = f32_dot(att_in[...].reshape(SIDE * rows, width), proj_w[...])
+    branch = branch.reshape(SIDE, SIDE, SLOTS, width)
+    for c in range(SIDE):
+        branch_out[c] = branch[:, c].reshape(rows, width)
+    for d in range(1, SIDE):
+        c = other(t, d)
+        send(remote(branch_out.at[c], branch_in.at[d - 1], 5, d, d, r, c))
+    total = branch_out[t]
+    for d in range(SIDE):
+        q = other(r, d)
+        receive(res_in.at[q], 1, q, on_diagonal if d == 0 else None)
+    residual = res_in[...].reshape(rows, width).astype(jnp.float32)
+    for d in range(1, SIDE):
+        receive(branch_in.at[d - 1], 5, d)
+        total = total + branch_in[d - 1]
+    hid_out[...] = (residual + total).astype(jnp.bfloat16)
+    for d in range(SIDE):
+        unless = on_diagonal if d == 0 else None
+        send(remote(hid_out, hid_in.at[r], 6, d, r, t, other(t, d)), unless)
+
+    @pl.when(on_diagonal)
+    def _():
+        hid_in[r] = hid_out[...]
+
+    loads[2].wait()
+    for d in range(SIDE):
+        q = other(r, d)
+        receive(hid_in.at[q], 6, q, on_diagonal if d == 0 else None)
+
+    merged = chunk_norm([hid_in[c].astype(jnp.float32) for c in range(SIDE)], merge_gain)
+    before = f32_dot(merged[0], fc1_w[0:width])
+    for c in range(1, SIDE):
+        before = before + f32_dot(merged[c], fc1_w[c * width : (c + 1) * width])
+    for q in range(SIDE):
+        pre_own[q] = before[q * SLOTS : (q + 1) * SLOTS]
+        pre_out[q] = before[q * SLOTS : (q + 1) * SLOTS].astype(jnp.bfloat16)
+    for d in range(1, SIDE):
+        p = other(r, d)
+        send(remote(pre_out.at[p], pre_in.at[d - 1], 7, d, d, p, t))
+    total = pre_own[r]
+    for d in range(1, SIDE):
+        receive(pre_in.at[d - 1], 7, d)
+        total = total + pre_in[d - 1].astype(jnp.float32)
+    act_out[...] = (0.5 * total * (1.0 + lax.erf(total * (0.5**0.5)))).astype(jnp.bfloat16)
+    for d in range(1, SIDE):
+        send(remote(act_out, act_in.at[r], 8, d, d, other(r, d), t))
+    act_in[r] = act_out[...]
+    table = image_table(counts, image_request, image_position, request_len, token_rows)
+    slot_i = iota((SIDE * SLOTS, SIDE * SLOTS), 0)
+    row_j = iota((SIDE * SLOTS, SIDE * SLOTS), 1)
+    pick = jnp.zeros(slot_i.shape, jnp.float32)
+    for source, _, run, owner, base in table:
+        offset = row_j - source
+        hit = (slot_i - (owner * SLOTS + base) == offset) & (offset >= 0) & (offset < run)
+        pick = jnp.where(hit, 1.0, pick)
+    pick = pick.astype(jnp.bfloat16)
+    loads[3].wait()
+    for d in range(1, SIDE):
+        receive(act_in.at[other(r, SIDE - d)], 8, d)
+
+    active = act_in[...].reshape(SIDE * SLOTS, act_in.shape[2])
+    picked = f32_dot(pick, active).astype(jnp.bfloat16)
+    outward = f32_dot(picked, fc2_w[...]).astype(jnp.bfloat16)
+    for q in range(SIDE):
+        vis_out[q] = outward[q * SLOTS : (q + 1) * SLOTS]
+    for d in range(SIDE):
+        q = other(r, d)
+        unless = on_diagonal if d == 0 else None
+        send(remote(vis_out.at[q], vis_in.at[t], 9, d, t, q, r), unless)
+
+    @pl.when(on_diagonal)
+    def _():
+        vis_in[t] = vis_out[r]
+
+    loads[4].wait()
+    for d in range(SIDE):
+        q = other(t, d)
+        receive(vis_in.at[q], 9, q, on_diagonal if d == 0 else None)
+    visual = vis_in[0].astype(jnp.float32)
+    for q in range(1, SIDE):
+        visual = visual + vis_in[q].astype(jnp.float32)
+    visual = visual.astype(jnp.bfloat16).astype(jnp.float32)
+    squares = jnp.sum(visual * visual, axis=1, keepdims=True)
+    sq_out[...] = jnp.broadcast_to(squares, sq_out.shape)
+    for d in range(1, SIDE):
+        send(remote(sq_out, sq_in.at[d - 1], 10, d, d, r, other(t, d)))
+    projected = f32_dot((visual * rms_gain[...]).astype(jnp.bfloat16), kv_w[...])
+    row_out[...] = projected.astype(jnp.bfloat16)
+    for d in range(1, SIDE):
+        send(remote(row_out, row_in.at[d - 1], 11, d, d, r, other(t, d)))
+    total = projected
+    squares = sq_out[...]
+    for d in range(1, SIDE):
+        receive(sq_in.at[d - 1], 10, d)
+        squares = squares + sq_in[d - 1]
+        receive(row_in.at[d - 1], 11, d)
+        total = total + row_in[d - 1].astype(jnp.float32)
+    total = total * lax.rsqrt(squares[:, :1] / (SIDE * visual.shape[1]) + epsilon)
+    share = placed_ref.shape[0]
+    place_i = iota((share, SLOTS), 0) + r * token_rows + t * share
+    place_k = iota((share, SLOTS), 1)
+    place = jnp.zeros((share, SLOTS), jnp.float32)
+    for _, first, run, owner, base in table:
+        offset = place_i - first
+        hit = (owner == r) & (place_k - base == offset) & (offset >= 0) & (offset < run)
+        place = jnp.where(hit, 1.0, place)
+    placed_ref[...] = jnp.dot(
+        place, total, preferred_element_type=jnp.float32, precision=lax.Precision.HIGHEST
+    )
+    for wait in pending:
+        wait()
+
+
+def vision_rows(
+    request_len,
+    token_rows,
+    patch_counts,
+    image_request,
+    image_position,
+    patches,
+    vit_gain,
+    merge_gain,
+    rms_gain,
+    qkv_weight,
+    proj_weight,
+    fc1_weight,
+    fc2_weight,
+    kv_flat,
+):
+    rows, width = patches.shape
+    hidden_w = fc1_weight.shape[1]
+    share_w, kv_width = kv_flat.shape
+    bf16, f32 = jnp.bfloat16, jnp.float32
+    n = SIDE
+    smem = pl.BlockSpec(memory_space=pltpu.SMEM)
+    vmem = pl.BlockSpec(memory_space=pltpu.VMEM)
+    anywhere = pl.BlockSpec(memory_space=pl.ANY)
+    buffers = [
+        ((3, width, width), bf16),
+        (proj_weight.shape, bf16),
+        (fc1_weight.shape, bf16),
+        (fc2_weight.shape, bf16),
+        (kv_flat.shape, bf16),
+        None,
+        ((n, rows, width), bf16),
+        ((n, SLOTS, width), bf16),
+        ((n, SLOTS, width), bf16),
+        ((n, rows, width), bf16),
+        ((n, rows, width), bf16),
+        ((n, 3, rows, width), f32),
+        ((n, 3, rows, width), bf16),
+        ((n - 1, 3, rows, width), bf16),
+        ((rows, width), bf16),
+        ((n, rows, width), bf16),
+        ((n, rows, width), f32),
+        ((n - 1, rows, width), f32),
+        ((rows, width), bf16),
+        ((n, rows, width), bf16),
+        ((n, SLOTS, hidden_w), f32),
+        ((n, SLOTS, hidden_w), bf16),
+        ((n - 1, SLOTS, hidden_w), bf16),
+        ((SLOTS, hidden_w), bf16),
+        ((n, SLOTS, hidden_w), bf16),
+        ((n, SLOTS, share_w), bf16),
+        ((n, SLOTS, share_w), bf16),
+        ((SLOTS, kv_width), bf16),
+        ((n - 1, SLOTS, kv_width), bf16),
+        ((SLOTS, 128), f32),
+        ((n - 1, SLOTS, 128), f32),
+    ]
+    scratch = [
+        pltpu.SemaphoreType.DMA((5,)) if b is None else pltpu.VMEM(*b) for b in buffers
+    ] + [pltpu.SemaphoreType.DMA((12, n)), pltpu.SemaphoreType.DMA((12, n))]
+    return pl.pallas_call(
+        functools.partial(vision_kernel, request_len, token_rows),
+        out_shape=jax.ShapeDtypeStruct((token_rows // n, kv_width), f32),
+        in_specs=[smem] * 3 + [vmem] * 4 + [anywhere] * 5,
+        out_specs=vmem,
+        scratch_shapes=scratch,
+        compiler_params=pltpu.CompilerParams(
+            collective_id=0, has_side_effects=True, vmem_limit_bytes=48 * 1024 * 1024
+        ),
+        cost_estimate=pl.CostEstimate(
+            flops=2 * 10**9, bytes_accessed=20 * 10**6, transcendentals=10**5
+        ),
+    )(
+        patch_counts,
+        image_request,
+        image_position,
+        patches,
+        vit_gain.reshape(n, width),
+        merge_gain.reshape(n, width),
+        rms_gain.reshape(1, share_w),
+        jnp.transpose(qkv_weight, (1, 0, 2)),
+        proj_weight,
+        fc1_weight,
+        fc2_weight,
+        kv_flat,
+    )
+
+
+def square_body(
+    patches,
+    patch_counts,
+    image_request,
+    image_position,
+    request_lengths,
+    vit_gain,
+    qkv_weight,
+    proj_weight,
+    merge_gain,
+    fc1_weight,
+    fc2_weight,
+    text_rows,
+    rms_gain,
+    kv_weight,
+    kv_scale,
+):
+    req_index = lax.axis_index("req")
+    tp_index = lax.axis_index("tp")
+    token_rows, share_w = text_rows.shape
+    request_len = SIDE * token_rows // request_lengths.shape[0]
+    share_rows = token_rows // SIDE
+    kv_flat = kv_weight.reshape(share_w, -1)
+    wide = text_rows.astype(jnp.float32)
+    part = f32_dot((wide * rms_gain).astype(jnp.bfloat16), kv_flat).astype(jnp.bfloat16)
+    text_sum = lax.psum_scatter(part, "tp", scatter_dimension=0, tiled=True)
+    squares = lax.psum_scatter(
+        jnp.sum(wide * wide, axis=1), "tp", scatter_dimension=0, tiled=True
+    )
+    placed = vision_rows(
+        request_len,
+        token_rows,
+        patch_counts,
+        image_request,
+        image_position,
+        patches,
+        vit_gain,
+        merge_gain,
+        rms_gain,
+        qkv_weight,
+        proj_weight,
+        fc1_weight,
+        fc2_weight,
+        kv_flat,
+    )
+    row_ids = (
+        req_index * token_rows + tp_index * share_rows + jnp.arange(share_rows, dtype=jnp.int32)
+    )
+    runs = patch_counts // 4
+    firsts = (image_request * request_len + image_position).reshape(-1)
+    offsets = row_ids[:, None] - firsts[None, :]
+    taken = jnp.any((offsets >= 0) & (offsets < runs.reshape(-1)[None, :]), axis=1)
+    plain = text_sum.astype(jnp.float32) * lax.rsqrt(squares[:, None] / D + epsilon)
+    stacked = jnp.where(taken[:, None], placed, plain).reshape(share_rows, 2, -1)
+    positions = row_ids % request_len
+    live_rows = positions < request_lengths[row_ids // request_len]
+    return finish_cache(stacked, positions, live_rows, kv_scale)
+
+
 def solution(mesh):
     placed = (
         P(("groups", "req"), "tp"),
@@ -209,8 +702,9 @@
         P("tp", None, None),
         P(),
     )
+    square = mesh.shape["req"] == SIDE and mesh.shape["tp"] == SIDE
     return jax.shard_map(
-        body,
+        square_body if square else general_body,
         mesh=mesh,
         in_specs=placed,
         out_specs=P(("groups", "req", "tp"), None, None),

time: 304 us -> 135 us (0.44)
  waiting for transfers between devices: 142 us -> 0.04 us
  Pallas kernels: 0 us -> 81.3 us
  blocking collectives: 73.8 us -> 6.38 us
  matrix products: 23.5 us -> 9.12 us
  local copies, waits for them, and re-layouts: 27.3 us -> 16.2 us
  other arithmetic: 16.8 us -> 7.86 us
  starting transfers between devices: 4.92 us -> 0.01 us
    reduce_scatter x3 -> x1, waiting for transfers between devices: 85.4 us -> 0.02 us  [square_body(): text_sum = lax.psum_scatter(part, 'tp', scatter_dimension=0, tiled=True)]
    pallas_call x0 -> x1, Pallas kernels: none -> 81.3 us  [vision_rows(): pl.pallas_call(functools.partial(vision_kernel, request_len, token_rows),...]
    all_gather x3 -> x0, blocking collectives: 55.3 us -> none  [the longest x1 37.6 us: body(): lax.all_gather(proj_weight, 'req', axis=1, tiled=True)]
    psum x1 -> x0, waiting for transfers between devices: 27 us -> none  [body(): branch_total = lax.psum(branch, 'tp')]
    all_gather x1 -> x0, waiting for transfers between devices: 24.8 us -> none  [body(): lax.all_gather(qkv_weight, 'req', axis=0, tiled=True)]
    dot_general x7 -> x1, matrix products: 23.5 us -> 9.12 us  [f32_dot(): return jnp.dot(left, right, preferred_element_type=jnp.float32)]
    all_to_all x1 -> x0, blocking collectives: 12.7 us -> none  [body(): lax.all_to_all(sending, 'req', split_axis=0, concat_axis=1, tiled=True)]
    unnamed x21 -> x33, local copies, waits for them, and re-layouts: 4.27 us -> 13.1 us
  transfers between devices with their start and end apart: 6 -> 1, of which waited for: 6 -> 0; matrix products, arithmetic and copies ran while one was open for 6% -> 4% of each run, Pallas kernels for 0% -> 60%
where the time goes in v1:
time: 135 us
  Pallas kernels  81.3 us (60%)
  local copies, waits for them, and re-layouts  16.2 us (12%)
  between operations  14.3 us (11%)
  matrix products  9.12 us (7%)
  other arithmetic  7.86 us (6%)
  blocking collectives  6.38 us (5%)
    pallas_call x1, Pallas kernels, vision_rows(): pl.pallas_call(functools.partial(vision_kernel, request_len, token_rows),...  81.3 us
    unnamed x33, local copies, waits for them, and re-layouts  13.1 us
    dot_general x1, matrix products, f32_dot(): return jnp.dot(left, right, preferred_element_type=jnp.float32)  9.12 us
    unnamed x1, blocking collectives  6.38 us
  transfers between devices with their start and end apart: 1, of which 0 were waited for; matrix products, arithmetic and copies ran while one was open for 4% of the time, Pallas kernels for 60%

profile of v1, /device:TPU:1, one launch (start us, length us, event | category | flops | bytes accessed | tf_op | source)
XLA Modules:
  0.0 135.2 jit_solution(18403279008336439254)
XLA Ops:
  6.5 0.0 reduce-scatter.2.cloned.1.call-start
  6.5 10.3 %copy.36 = bf16[256,8,2,1024]{3,1,2,0:T(8,128)(2,1)} copy(bf16[256,8,2,1024]{3,2,1,0:T(2,128)(2,1)} %bitcast.20) | data formatting | bytes 16777216
  16.8 0.0 copy-done.4
  16.8 0.0 copy-done.5
  16.9 0.0 copy-start.10
  16.9 0.0 copy-start.6
  16.9 0.0 copy-start.7
  16.9 0.0 copy-start.12
  16.9 0.0 copy-start.13
  16.9 9.1 %convolution_convert_fusion = bf16[512,2048]{1,0:T(8,128)(2,1)} fusion(bf16[2048,2048]{1,0:T(8,128)(2,1)} %bitcast.18, bf16[512,2048]{1,0:T(8,128)(2,1)S(1)} %copy-done.5, f32[2048]{0:T(1024)S(1)} %copy-done.4), kind=kOutput, calls=%fused_computation.4 | convolution fusion | flops 4299161600 | bytes 12591104 | tf_op jit(solution)/shard_map/dot_general | solution.py:203
  26.0 0.0 reduce-scatter.2.cloned.1.call-update
  26.1 0.0 copy-done.11
  26.1 0.1 copy.33.counts
  26.2 0.1 copy.32
  26.3 0.1 lt.37
  26.4 0.0 copy-done.9
  26.4 0.1 copy.34.image_request
  26.5 0.0 copy-done.10
  26.5 0.1 copy.35.image_position
  26.6 0.1 copy.31
  26.7 0.1 sub.30
  26.8 0.0 copy-done.6
  26.8 0.1 reshape.181.vit_gain
  26.8 0.0 copy-done.7
  26.8 0.1 reshape.182.merge_gain
  26.9 0.0 copy-done.12
  26.9 0.1 broadcast_in_dim.23
  27.0 0.1 min.14
  27.1 0.0 copy-done.13
  27.1 0.6 dynamic-slice
  28.4 0.5 fusion.1
  28.8 6.4 %all-reduce = f32[512]{0:T(512)S(1)} all-reduce(f32[512]{0:T(512)S(1)} %fusion.1), channel_id=3, replica_groups=mesh['groups'=2,'req'=4,'tp'=4] {'tp'}, use_global_device_ids=true, to_apply=%region_3.4.clone | all-reduce | flops 512 | bytes 4096
  35.3 0.1 fusion.13
  35.3 0.6 fusion.15
  36.0 2.5 %fusion.10 = pred[128]{0:T(512)(128)(4,1)S(1)} fusion(s32[]{:T(128)} %bitcast, s32[]{:T(128)} %bitcast.1, s32[]{:T(128)} %bitcast.3, s32[]{:T(128)} %bitcast.2, s32[]{:T(128)S(6)} %add.83), kind=kLoop, calls=%fused_computation.37 | loop fusion | flops 4864 | bytes 148 | tf_op jit(solution)/shard_map/lt | solution.py:683
  38.5 0.1 fusion.8
  38.6 0.0 copy-start
  38.6 1.9 %copy-done = bf16[1280,1280]{1,0:T(8,128)(2,1)S(1)} copy-done((bf16[1280,1280]{1,0:T(8,128)(2,1)S(1)}, bf16[1280,1280]{1,0:T(8,128)(2,1)}, u32[]{:S(2)}) %copy-start) | copy-done | bytes 3276824
  40.6 81.3 %shard_map.145 = f32[128,2048]{1,0:T(8,128)S(1)} custom-call(s32[4,2]{1,0:T(4,128)S(1)} %copy.33.counts, s32[4,2]{1,0:T(4,128)S(1)} %copy.34.image_request, s32[4,2]{1,0:T(4,128)S(1)} %copy.35.image_position, bf16[64,320]{1,0:T(8,128)(2,1)S(1)} %copy-done.3, f32[4,320]{1,0:T(4,128)S(1)} %reshape.181.vit_gain, f32[4,320]{1,0:T(4,128)S(1)} %reshape.182.merge_gain, ...), custom_call_target="tpu_custom_call" | custom-call | flops 2000000000 | bytes 20000000 | tf_op jit(solution)/shard_map/pallas_call | solution.py:600
  121.8 0.3 multiply_cosine_fusion
  122.1 0.0 reduce-scatter.2.cloned.1.call-done
  122.2 1.3 multiply_select_fusion
  123.5 0.9 reshape.185
  124.4 0.4 slice.21
  124.8 0.5 slice.24
  125.3 0.3 multiply_subtract_fusion
  125.6 0.2 pad_maximum_fusion
  125.8 2.5 %fusion.6 = bf16[128,2,1024]{2,1,0:T(2,128)(2,1)} fusion(bf16[128,1,1024]{2,1,0:T(2,128)(2,1)S(1)} %slice.24, f32[128,1,1024]{2,1,0:T(1,128)S(1)} %bitcast.22, pred[128]{0:T(512)(128)(4,1)S(1)} %fusion.10, bf16[2,1024]{1,0:T(2,128)(2,1)S(1)} %neg.7, f32[2,1024]{1,0:T(2,128)S(1)} %min.14), kind=kLoop, calls=%fused_computation.10 | loop fusion | flops 2359296 | bytes 1323136 | tf_op jit(solution)/shard_map/convert_element_type | solution.py:83
  (19 shorter events, 0.1 us)
Async XLA Ops:
  6.5 115.6 %reduce-scatter.2.cloned.1.call-start = ((), (), s32[]{:S(2)}) async-start(), calls=%async_computation.1 | async-start | bytes 2621440 | tf_op jit(solution)/shard_map/reduce_scatter | solution.py:653
  6.5 10.3 %copy-start.4 = (f32[2048]{0:T(1024)S(1)}, f32[2048]{0:T(1024)}, u32[]{:S(2)}) copy-start(f32[2048]{0:T(1024)} %param.27) | copy-start | bytes 24580
  6.5 10.3 %copy-start.5 = (bf16[512,2048]{1,0:T(8,128)(2,1)S(1)}, bf16[512,2048]{1,0:T(8,128)(2,1)}, u32[]{:S(2)}) copy-start(bf16[512,2048]{1,0:T(8,128)(2,1)} %param.26) | copy-start | bytes 6291460
  16.8 9.2 %copy-start.11 = (s32[4,2]{0,1:T(2,128)S(1)}, s32[4,2]{0,1:T(2,128)}, u32[]{:S(2)}) copy-start(s32[4,2]{0,1:T(2,128)} %param.16) | copy-start | bytes 100
  16.8 9.5 %copy-start.9 = (s32[4,2]{0,1:T(2,128)S(1)}, s32[4,2]{0,1:T(2,128)}, u32[]{:S(2)}) copy-start(s32[4,2]{0,1:T(2,128)} %param.17) | copy-start | bytes 100
  16.9 9.6 %copy-start.10 = (s32[4,2]{0,1:T(2,128)S(1)}, s32[4,2]{0,1:T(2,128)}, u32[]{:S(2)}) copy-start(s32[4,2]{0,1:T(2,128)} %param.18) | copy-start | bytes 100
  16.9 9.9 %copy-start.6 = (f32[1280]{0:T(1024)S(1)}, f32[1280]{0:T(1024)}, u32[]{:S(2)}) copy-start(f32[1280]{0:T(1024)} %param.20) | copy-start | bytes 15364
  16.9 10.0 %copy-start.7 = (f32[1280]{0:T(1024)S(1)}, f32[1280]{0:T(1024)}, u32[]{:S(2)}) copy-start(f32[1280]{0:T(1024)} %param.23) | copy-start | bytes 15364
  16.9 10.0 %copy-start.12 = (f32[2,16]{1,0:T(2,128)S(1)}, f32[2,16]{1,0:T(2,128)}, u32[]{:S(2)}) copy-start(f32[2,16]{1,0:T(2,128)} %param.29) | copy-start | bytes 388
  16.9 10.2 %copy-start.13 = (u32[32]{0:T(128)S(1)}, u32[32]{0:T(128)}, u32[]{:S(2)}) copy-start(u32[32]{0:T(128)} %constant.81) | copy-start | bytes 388
  26.0 9.3 %copy-start.8 = (s32[4]{0:T(128)S(1)}, s32[4]{0:T(128)}, u32[]{:S(2)}) copy-start(s32[4]{0:T(128)} %param.19) | copy-start | bytes 52
  26.0 12.6 %copy-start.1 = (bf16[320,3,320]{2,0,1:T(8,128)(2,1)S(1)}, bf16[320,3,320]{2,0,1:T(8,128)(2,1)}, u32[]{:S(2)}) copy-start(bf16[320,3,320]{2,0,1:T(8,128)(2,1)} %param.21) | copy-start | bytes 1843204
  26.0 12.6 %copy-start.2 = (bf16[320,320]{1,0:T(8,128)(2,1)S(1)}, bf16[320,320]{1,0:T(8,128)(2,1)}, u32[]{:S(2)}) copy-start(bf16[320,320]{1,0:T(8,128)(2,1)} %proj_hbm.1) | copy-start | bytes 614404
  26.0 12.6 %copy-start.3 = (bf16[64,320]{1,0:T(8,128)(2,1)S(1)}, bf16[64,320]{1,0:T(8,128)(2,1)}, u32[]{:S(2)}) copy-start(bf16[64,320]{1,0:T(8,128)(2,1)} %patches.1) | copy-start | bytes 122884
  38.6 1.9 %copy-start = (bf16[1280,1280]{1,0:T(8,128)(2,1)S(1)}, bf16[1280,1280]{1,0:T(8,128)(2,1)}, u32[]{:S(2)}) copy-start(bf16[1280,1280]{1,0:T(8,128)(2,1)} %fc1_hbm.1) | copy-start | bytes 9830404
Sparse Core Ops, SparseCore 0:
  26.2 35.6 reduce-scatter.1

commit v2 on v1

--- a/solution.py
+++ b/solution.py
@@ -241,12 +241,14 @@
     fc1_hbm,
     fc2_hbm,
     kv_hbm,
+    text_hbm,
     placed_ref,
     qkv_w,
     proj_w,
     fc1_w,
     fc2_w,
     kv_w,
+    text_v,
     load_sem,
     patch_all,
     res_out,
@@ -273,6 +275,12 @@
     row_in,
     sq_out,
     sq_in,
+    tsq_out,
+    tsq_in,
+    text_keep,
+    text_out,
+    text_in,
+    sums,
     send_sem,
     recv_sem,
 ):
@@ -286,7 +294,14 @@
 
     loads = []
     for k, (src, dst) in enumerate(
-        ((qkv_hbm, qkv_w), (proj_hbm, proj_w), (fc1_hbm, fc1_w), (fc2_hbm, fc2_w), (kv_hbm, kv_w))
+        (
+            (qkv_hbm, qkv_w),
+            (text_hbm, text_v),
+            (kv_hbm, kv_w),
+            (proj_hbm, proj_w),
+            (fc1_hbm, fc1_w),
+            (fc2_hbm, fc2_w),
+        )
     ):
         copy = pltpu.make_async_copy(src, dst, load_sem.at[k])
         copy.start()
@@ -353,6 +368,18 @@
     def _():
         res_in[r] = res_out[t]
 
+    share = placed_ref.shape[0]
+
+    def text_chunk(c):
+        return text_v[pl.ds(pl.multiple_of(c * share, share), share)].astype(jnp.float32)
+
+    loads[1].wait()
+    for c in range(SIDE):
+        wide = text_chunk(c)
+        column = jnp.sum(wide * wide, axis=1, keepdims=True)
+        tsq_out[c] = jnp.transpose(jnp.broadcast_to(column, (share, share)))[:8]
+    for d in range(1, SIDE):
+        send(remote(tsq_out, tsq_in.at[d - 1], 12, d, d, r, other(t, d)))
     for d in range(1, SIDE):
         receive(patch_all.at[other(t, SIDE - d)], 0, d)
 
@@ -390,6 +417,32 @@
     for d in range(1, SIDE):
         p = other(r, d)
         send(remote(part_out.at[p], part_in.at[d - 1], 3, d, d, p, t))
+
+    for d in range(1, SIDE):
+        receive(tsq_in.at[d - 1], 12, d)
+    for c in range(SIDE):
+        tsq_out_sum = tsq_out[c]
+        for d in range(1, SIDE):
+            tsq_out_sum = tsq_out_sum + tsq_in[d - 1, c]
+        sums[c] = tsq_out_sum
+    loads[2].wait()
+    mate = t + 1 - 2 * lax.rem(t, 2)
+    across = other(t, 2)
+    columns = text_v.shape[1]
+
+    def text_part(c):
+        squares = jnp.transpose(jnp.broadcast_to(sums[c][:1], (share, share)))[:, :1]
+        inverse = lax.rsqrt(squares / (SIDE * columns) + epsilon)
+        scaled = (text_chunk(c) * inverse * rms_gain[...]).astype(jnp.bfloat16)
+        return f32_dot(scaled, kv_w[...])
+
+    text_out[0] = text_part(other(mate, 2)).astype(jnp.bfloat16)
+    send(remote(text_out.at[0], text_in.at[0], 13, 0, 0, r, mate))
+    text_keep[...] = text_part(across)
+    receive(text_in.at[0], 13, 0)
+    text_out[1] = (text_keep[...] + text_in[0].astype(jnp.float32)).astype(jnp.bfloat16)
+    send(remote(text_out.at[1], text_in.at[1], 13, 1, 1, r, across))
+
     total = part_own[r]
     for d in range(1, SIDE):
         receive(part_in.at[d - 1], 3, d)
@@ -420,7 +473,9 @@
     for d in range(1, SIDE):
         send(remote(att_out, att_in.at[r], 4, d, d, other(r, d), t))
     att_in[r] = att_out[...]
-    loads[1].wait()
+    text_out[2] = text_part(mate).astype(jnp.bfloat16)
+    send(remote(text_out.at[2], text_in.at[2], 13, 2, 2, r, mate))
+    loads[3].wait()
     for d in range(1, SIDE):
         receive(att_in.at[other(r, SIDE - d)], 4, d)
 
@@ -448,7 +503,8 @@
     def _():
         hid_in[r] = hid_out[...]
 
-    loads[2].wait()
+    text_keep[...] = text_part(t)
+    loads[4].wait()
     for d in range(SIDE):
         q = other(r, d)
         receive(hid_in.at[q], 6, q, on_diagonal if d == 0 else None)
@@ -480,7 +536,7 @@
         hit = (slot_i - (owner * SLOTS + base) == offset) & (offset >= 0) & (offset < run)
         pick = jnp.where(hit, 1.0, pick)
     pick = pick.astype(jnp.bfloat16)
-    loads[3].wait()
+    loads[5].wait()
     for d in range(1, SIDE):
         receive(act_in.at[other(r, SIDE - d)], 8, d)
 
@@ -498,7 +554,6 @@
     def _():
         vis_in[t] = vis_out[r]
 
-    loads[4].wait()
     for d in range(SIDE):
         q = other(t, d)
         receive(vis_in.at[q], 9, q, on_diagonal if d == 0 else None)
@@ -522,7 +577,6 @@
         receive(row_in.at[d - 1], 11, d)
         total = total + row_in[d - 1].astype(jnp.float32)
     total = total * lax.rsqrt(squares[:, :1] / (SIDE * visual.shape[1]) + epsilon)
-    share = placed_ref.shape[0]
     place_i = iota((share, SLOTS), 0) + r * token_rows + t * share
     place_k = iota((share, SLOTS), 1)
     place = jnp.zeros((share, SLOTS), jnp.float32)
@@ -530,9 +584,15 @@
         offset = place_i - first
         hit = (owner == r) & (place_k - base == offset) & (offset >= 0) & (offset < run)
         place = jnp.where(hit, 1.0, place)
-    placed_ref[...] = jnp.dot(
+    placed = jnp.dot(
         place, total, preferred_element_type=jnp.float32, precision=lax.Precision.HIGHEST
     )
+    taken = jnp.sum(place, axis=1, keepdims=True) > 0.5
+    plain = text_keep[...]
+    for k in (1, 2):
+        receive(text_in.at[k], 13, k)
+        plain = plain + text_in[k].astype(jnp.float32)
+    placed_ref[...] = jnp.where(taken, placed, plain)
     for wait in pending:
         wait()
 
@@ -552,12 +612,14 @@
     fc1_weight,
     fc2_weight,
     kv_flat,
+    text_rows,
 ):
     rows, width = patches.shape
     hidden_w = fc1_weight.shape[1]
     share_w, kv_width = kv_flat.shape
     bf16, f32 = jnp.bfloat16, jnp.float32
     n = SIDE
+    share = token_rows // n
     smem = pl.BlockSpec(memory_space=pltpu.SMEM)
     vmem = pl.BlockSpec(memory_space=pltpu.VMEM)
     anywhere = pl.BlockSpec(memory_space=pl.ANY)
@@ -567,6 +629,7 @@
         (fc1_weight.shape, bf16),
         (fc2_weight.shape, bf16),
         (kv_flat.shape, bf16),
+        (text_rows.shape, bf16),
         None,
         ((n, rows, width), bf16),
         ((n, SLOTS, width), bf16),
@@ -593,21 +656,27 @@
         ((n - 1, SLOTS, kv_width), bf16),
         ((SLOTS, 128), f32),
         ((n - 1, SLOTS, 128), f32),
+        ((n, 8, share), f32),
+        ((n - 1, n, 8, share), f32),
+        ((share, kv_width), f32),
+        ((3, share, kv_width), bf16),
+        ((3, share, kv_width), bf16),
+        ((n, 8, share), f32),
     ]
     scratch = [
-        pltpu.SemaphoreType.DMA((5,)) if b is None else pltpu.VMEM(*b) for b in buffers
-    ] + [pltpu.SemaphoreType.DMA((12, n)), pltpu.SemaphoreType.DMA((12, n))]
+        pltpu.SemaphoreType.DMA((6,)) if b is None else pltpu.VMEM(*b) for b in buffers
+    ] + [pltpu.SemaphoreType.DMA((14, n)), pltpu.SemaphoreType.DMA((14, n))]
     return pl.pallas_call(
         functools.partial(vision_kernel, request_len, token_rows),
         out_shape=jax.ShapeDtypeStruct((token_rows // n, kv_width), f32),
-        in_specs=[smem] * 3 + [vmem] * 4 + [anywhere] * 5,
+        in_specs=[smem] * 3 + [vmem] * 4 + [anywhere] * 6,
         out_specs=vmem,
         scratch_shapes=scratch,
         compiler_params=pltpu.CompilerParams(
             collective_id=0, has_side_effects=True, vmem_limit_bytes=48 * 1024 * 1024
         ),
         cost_estimate=pl.CostEstimate(
-            flops=2 * 10**9, bytes_accessed=20 * 10**6, transcendentals=10**5
+            flops=6 * 10**9, bytes_accessed=22 * 10**6, transcendentals=10**5
         ),
     )(
         patch_counts,
@@ -622,6 +691,7 @@
         fc1_weight,
         fc2_weight,
         kv_flat,
+        text_rows,
     )
 
 
@@ -648,12 +718,6 @@
     request_len = SIDE * token_rows // request_lengths.shape[0]
     share_rows = token_rows // SIDE
     kv_flat = kv_weight.reshape(share_w, -1)
-    wide = text_rows.astype(jnp.float32)
-    part = f32_dot((wide * rms_gain).astype(jnp.bfloat16), kv_flat).astype(jnp.bfloat16)
-    text_sum = lax.psum_scatter(part, "tp", scatter_dimension=0, tiled=True)
-    squares = lax.psum_scatter(
-        jnp.sum(wide * wide, axis=1), "tp", scatter_dimension=0, tiled=True
-    )
     placed = vision_rows(
         request_len,
         token_rows,
@@ -669,16 +733,12 @@
         fc1_weight,
         fc2_weight,
         kv_flat,
+        text_rows,
     )
     row_ids = (
         req_index * token_rows + tp_index * share_rows + jnp.arange(share_rows, dtype=jnp.int32)
     )
-    runs = patch_counts // 4
-    firsts = (image_request * request_len + image_position).reshape(-1)
-    offsets = row_ids[:, None] - firsts[None, :]
-    taken = jnp.any((offsets >= 0) & (offsets < runs.reshape(-1)[None, :]), axis=1)
-    plain = text_sum.astype(jnp.float32) * lax.rsqrt(squares[:, None] / D + epsilon)
-    stacked = jnp.where(taken[:, None], placed, plain).reshape(share_rows, 2, -1)
+    stacked = placed.reshape(share_rows, 2, -1)
     positions = row_ids % request_len
     live_rows = positions < request_lengths[row_ids // request_len]
     return finish_cache(stacked, positions, live_rows, kv_scale)

time: 135 us -> 103 us (0.76)
  between operations: 14.3 us -> 0.16 us
  matrix products: 9.12 us -> 0 us
  blocking collectives: 6.38 us -> 0 us
  other arithmetic: 7.86 us -> 5.83 us
    dot_general x1 -> x0, matrix products: 9.12 us -> none  [f32_dot(): return jnp.dot(left, right, preferred_element_type=jnp.float32)]
    unnamed x1 -> x0, blocking collectives: 6.38 us -> none
    unnamed x33 -> x18, local copies, waits for them, and re-layouts: 13.1 us -> 12.6 us
  transfers between devices with their start and end apart: 1 -> 0, of which waited for: 0 -> 0; matrix products, arithmetic and copies ran while one was open for 4% -> 0% of each run, Pallas kernels for 60% -> 0%
where the time goes in v2:
time: 103 us
  Pallas kernels  80.1 us (78%)
  local copies, waits for them, and re-layouts  16.8 us (16%)
  other arithmetic  5.83 us (6%)
    pallas_call x1, Pallas kernels, vision_rows(): pl.pallas_call(functools.partial(vision_kernel, request_len, token_rows),...  80.1 us
    unnamed x18, local copies, waits for them, and re-layouts  12.6 us
    lt x1, other arithmetic, square_body(): live_rows = positions < request_lengths[row_ids // request_len]  2.54 us
    convert_element_type x1, other arithmetic, finish_cache(): jnp.where(live_rows[:, None, None], clipped, 0.0).astype(jnp.bfloat16)  2.48 us

profile of v2, /device:TPU:1, one launch (start us, length us, event | category | flops | bytes accessed | tf_op | source)
XLA Modules:
  0.0 102.9 jit_solution(15753885337793830300)
XLA Ops:
  0.0 0.8 copy.16.counts
  0.8 0.8 copy.17.image_request
  1.5 0.8 copy.18.image_position
  2.3 0.8 reshape.171.vit_gain
  3.1 0.8 reshape.172.merge_gain
  3.8 0.0 copy-start
  3.8 0.0 copy-start.1
  3.8 0.0 copy-start.2
  3.8 0.0 copy-start.3
  3.9 0.0 copy-start.4
  3.9 10.3 %copy.19 = bf16[256,8,2,1024]{3,1,2,0:T(8,128)(2,1)} copy(bf16[256,8,2,1024]{3,2,1,0:T(2,128)(2,1)} %bitcast.16) | data formatting | bytes 16777216
  14.2 0.0 copy-done
  14.2 0.0 copy-done.1
  14.2 0.0 copy-done.2
  14.2 0.0 copy-done.3
  14.2 0.0 copy-done.4
  14.2 80.1 %shard_map.145 = f32[128,2048]{1,0:T(8,128)S(1)} custom-call(s32[4,2]{1,0:T(4,128)S(1)} %copy.16.counts, s32[4,2]{1,0:T(4,128)S(1)} %copy.17.image_request, s32[4,2]{1,0:T(4,128)S(1)} %copy.18.image_position, bf16[64,320]{1,0:T(8,128)(2,1)S(1)} %copy-done.3, f32[4,320]{1,0:T(4,128)S(1)} %reshape.171.vit_gain, f32[4,320]{1,0:T(4,128)S(1)} %reshape.172.merge_gain, ...), custom_call_target="tpu_custom_call" | custom-call | flops 6000000000 | bytes 22000000 | tf_op jit(solution)/shard_map/pallas_call | solution.py:669
  94.3 0.0 copy-start.5
  94.3 0.0 copy-start.6
  94.3 0.9 reshape.175
  95.2 0.5 slice.24
  95.8 0.4 slice.21
  96.2 0.3 multiply_cosine_fusion
  96.5 0.3 multiply_subtract_fusion
  96.8 0.2 pad_maximum_fusion
  97.0 0.0 copy-done.5
  97.0 0.7 fusion.7
  97.6 2.5 %fusion.4 = pred[128]{0:T(512)(128)(4,1)S(1)} fusion(s32[]{:T(128)} %bitcast, s32[]{:T(128)} %bitcast.1, s32[]{:T(128)} %bitcast.3, s32[]{:T(128)} %bitcast.2, s32[]{:T(128)S(6)} %add.65), kind=kLoop, calls=%fused_computation.21 | loop fusion | flops 4864 | bytes 148 | tf_op jit(solution)/shard_map/lt | solution.py:743
  100.2 0.0 copy-done.6
  100.2 0.1 broadcast_in_dim.26
  100.3 0.1 min.14
  100.4 2.5 %fusion.2 = bf16[128,2,1024]{2,1,0:T(2,128)(2,1)} fusion(bf16[128,1,1024]{2,1,0:T(2,128)(2,1)S(1)} %slice.24, f32[128,1,1024]{2,1,0:T(1,128)S(1)} %bitcast.19, pred[128]{0:T(512)(128)(4,1)S(1)} %fusion.4, bf16[2,1024]{1,0:T(2,128)(2,1)S(1)} %neg.7, f32[2,1024]{1,0:T(2,128)S(1)} %min.14), kind=kLoop, calls=%fused_computation.3 | loop fusion | flops 2359296 | bytes 1323136 | tf_op jit(solution)/shard_map/convert_element_type | solution.py:83
  (4 shorter events, 0.0 us)
Async XLA Ops:
  3.8 10.3 %copy-start = (bf16[512,2048]{1,0:T(8,128)(2,1)S(1)}, bf16[512,2048]{1,0:T(8,128)(2,1)}, u32[]{:S(2)}) copy-start(bf16[512,2048]{1,0:T(8,128)(2,1)} %text_hbm.1) | copy-start | bytes 6291460
  3.8 10.3 %copy-start.1 = (bf16[320,3,320]{2,0,1:T(8,128)(2,1)S(1)}, bf16[320,3,320]{2,0,1:T(8,128)(2,1)}, u32[]{:S(2)}) copy-start(bf16[320,3,320]{2,0,1:T(8,128)(2,1)} %param.21) | copy-start | bytes 1843204
  3.8 10.3 %copy-start.2 = (bf16[320,320]{1,0:T(8,128)(2,1)S(1)}, bf16[320,320]{1,0:T(8,128)(2,1)}, u32[]{:S(2)}) copy-start(bf16[320,320]{1,0:T(8,128)(2,1)} %proj_hbm.1) | copy-start | bytes 614404
  3.8 10.3 %copy-start.3 = (bf16[64,320]{1,0:T(8,128)(2,1)S(1)}, bf16[64,320]{1,0:T(8,128)(2,1)}, u32[]{:S(2)}) copy-start(bf16[64,320]{1,0:T(8,128)(2,1)} %patches.1) | copy-start | bytes 122884
  3.9 10.3 %copy-start.4 = (f32[2048]{0:T(1024)S(1)}, f32[2048]{0:T(1024)}, u32[]{:S(2)}) copy-start(f32[2048]{0:T(1024)} %param.27) | copy-start | bytes 24580
  94.3 2.7 %copy-start.5 = (s32[4]{0:T(128)S(1)}, s32[4]{0:T(128)}, u32[]{:S(2)}) copy-start(s32[4]{0:T(128)} %param.19) | copy-start | bytes 52
  94.3 5.9 %copy-start.6 = (f32[2,16]{1,0:T(2,128)S(1)}, f32[2,16]{1,0:T(2,128)}, u32[]{:S(2)}) copy-start(f32[2,16]{1,0:T(2,128)} %param.29) | copy-start | bytes 388

commit v3 on v2

--- a/solution.py
+++ b/solution.py
@@ -226,23 +226,25 @@
 SIDE = 4
 
 
-def vision_kernel(
+def cell_kernel(
     request_len,
     token_rows,
-    counts,
-    image_request,
-    image_position,
+    tables,
+    lengths,
     patches,
     vit_gain,
     merge_gain,
     rms_gain,
+    cosines,
+    sines,
+    limits,
     qkv_hbm,
     proj_hbm,
     fc1_hbm,
     fc2_hbm,
     kv_hbm,
     text_hbm,
-    placed_ref,
+    cache_ref,
     qkv_w,
     proj_w,
     fc1_w,
@@ -288,6 +290,7 @@
     t = lax.axis_index("tp")
     rows, width = patches.shape
     full = SIDE * width
+    counts, image_request, image_position = (tables.at[k] for k in range(3))
 
     def other(i, d):
         return lax.rem(i + d, SIDE)
@@ -368,7 +371,7 @@
     def _():
         res_in[r] = res_out[t]
 
-    share = placed_ref.shape[0]
+    share = cache_ref.shape[0]
 
     def text_chunk(c):
         return text_v[pl.ds(pl.multiple_of(c * share, share), share)].astype(jnp.float32)
@@ -394,7 +397,7 @@
             total = total + jnp.sum(v * v, axis=1, keepdims=True)
         inverse = lax.rsqrt(total / full + epsilon)
         return [
-            (v * inverse * gains[c : c + 1, :]).astype(jnp.bfloat16)
+            (v * inverse * gains[:, c * width : (c + 1) * width]).astype(jnp.bfloat16)
             for c, v in enumerate(centred)
         ]
 
@@ -592,12 +595,25 @@
     for k in (1, 2):
         receive(text_in.at[k], 13, k)
         plain = plain + text_in[k].astype(jnp.float32)
-    placed_ref[...] = jnp.where(taken, placed, plain)
+    stacked = jnp.where(taken, placed, plain)
+    row_ids = iota((share, HEAD_DIM), 0) + r * token_rows + t * share
+    live = row_ids < 0
+    for k in range(lengths.shape[0]):
+        inside = row_ids - k * request_len
+        live = live | ((inside >= 0) & (inside < lengths[k]))
+    heads = cache_ref.shape[1] // HEAD_DIM
+    for h in range(heads):
+        part = stacked[:, h * HEAD_DIM : (h + 1) * HEAD_DIM]
+        if h < heads // 2:
+            part = part * cosines[...] + pltpu.roll(part, HEAD_DIM // 2, 1) * sines[...]
+        bound = limits[:, h * HEAD_DIM : (h + 1) * HEAD_DIM]
+        part = jnp.where(live, jnp.clip(part, -bound, bound), 0.0)
+        cache_ref[:, h * HEAD_DIM : (h + 1) * HEAD_DIM] = part.astype(jnp.bfloat16)
     for wait in pending:
         wait()
 
 
-def vision_rows(
+def cell_cache(
     request_len,
     token_rows,
     patch_counts,
@@ -613,6 +629,8 @@
     fc2_weight,
     kv_flat,
     text_rows,
+    request_lengths,
+    kv_scale,
 ):
     rows, width = patches.shape
     hidden_w = fc1_weight.shape[1]
@@ -620,6 +638,13 @@
     bf16, f32 = jnp.bfloat16, jnp.float32
     n = SIDE
     share = token_rows // n
+    first_row = lax.axis_index("req") * token_rows + lax.axis_index("tp") * share
+    positions = (first_row + jnp.arange(share, dtype=jnp.int32)) % request_len
+    half_dim = HEAD_DIM // 2
+    frequency = theta_base ** (-2.0 * jnp.arange(half_dim, dtype=jnp.float32) / HEAD_DIM)
+    angles = positions.astype(jnp.float32)[:, None] * frequency[None, :]
+    cosine = jnp.cos(angles)
+    sine = jnp.sin(angles)
     smem = pl.BlockSpec(memory_space=pltpu.SMEM)
     vmem = pl.BlockSpec(memory_space=pltpu.VMEM)
     anywhere = pl.BlockSpec(memory_space=pl.ANY)
@@ -667,9 +692,9 @@
         pltpu.SemaphoreType.DMA((6,)) if b is None else pltpu.VMEM(*b) for b in buffers
     ] + [pltpu.SemaphoreType.DMA((14, n)), pltpu.SemaphoreType.DMA((14, n))]
     return pl.pallas_call(
-        functools.partial(vision_kernel, request_len, token_rows),
-        out_shape=jax.ShapeDtypeStruct((token_rows // n, kv_width), f32),
-        in_specs=[smem] * 3 + [vmem] * 4 + [anywhere] * 6,
+        functools.partial(cell_kernel, request_len, token_rows),
+        out_shape=jax.ShapeDtypeStruct((share, kv_width), bf16),
+        in_specs=[smem] * 2 + [vmem] * 7 + [anywhere] * 6,
         out_specs=vmem,
         scratch_shapes=scratch,
         compiler_params=pltpu.CompilerParams(
@@ -679,13 +704,15 @@
             flops=6 * 10**9, bytes_accessed=22 * 10**6, transcendentals=10**5
         ),
     )(
-        patch_counts,
-        image_request,
-        image_position,
+        jnp.stack([patch_counts, image_request, image_position]),
+        request_lengths,
         patches,
-        vit_gain.reshape(n, width),
-        merge_gain.reshape(n, width),
+        vit_gain.reshape(1, n * width),
+        merge_gain.reshape(1, n * width),
         rms_gain.reshape(1, share_w),
+        jnp.concatenate([cosine, cosine], axis=1),
+        jnp.concatenate([-sine, sine], axis=1),
+        jnp.repeat(clip_level * kv_scale.reshape(1, -1), QGROUP, axis=1),
         jnp.transpose(qkv_weight, (1, 0, 2)),
         proj_weight,
         fc1_weight,
@@ -712,13 +739,11 @@
     kv_weight,
     kv_scale,
 ):
-    req_index = lax.axis_index("req")
-    tp_index = lax.axis_index("tp")
     token_rows, share_w = text_rows.shape
     request_len = SIDE * token_rows // request_lengths.shape[0]
     share_rows = token_rows // SIDE
     kv_flat = kv_weight.reshape(share_w, -1)
-    placed = vision_rows(
+    cache = cell_cache(
         request_len,
         token_rows,
         patch_counts,
@@ -734,14 +759,10 @@
         fc2_weight,
         kv_flat,
         text_rows,
-    )
-    row_ids = (
-        req_index * token_rows + tp_index * share_rows + jnp.arange(share_rows, dtype=jnp.int32)
-    )
-    stacked = placed.reshape(share_rows, 2, -1)
-    positions = row_ids % request_len
-    live_rows = positions < request_lengths[row_ids // request_len]
-    return finish_cache(stacked, positions, live_rows, kv_scale)
+        request_lengths,
+        kv_scale,
+    )
+    return cache.reshape(share_rows, 2, -1)
 
 
 def solution(mesh):

time: 103 us -> 97.4 us (0.946)
  other arithmetic: 5.83 us -> 1.12 us
  local copies, waits for them, and re-layouts: 16.8 us -> 15.4 us
    lt x1 -> x0, other arithmetic: 2.54 us -> none  [square_body(): live_rows = positions < request_lengths[row_ids // request_len]]
    convert_element_type x2 -> x1, other arithmetic: 2.5 us -> 0.01 us  [cell_cache(): angles = positions.astype(jnp.float32)[:, None] * frequency[None, :]]
    another operation x0 -> x3, local copies, waits for them, and re-layouts: none -> 2.29 us  [cell_cache(): jnp.stack([patch_counts, image_request, image_position])]
    unnamed x18 -> x13, local copies, waits for them, and re-layouts: 12.6 us -> 10.3 us
where the time goes in v3:
time: 97.4 us; the launch traced here: 97.1 us
  Pallas kernels  80.4 us (83%)
  local copies, waits for them, and re-layouts  15.4 us (16%)
  other arithmetic  1.12 us (1%)
    pallas_call x1, Pallas kernels, cell_cache(): pl.pallas_call(functools.partial(cell_kernel, request_len, token_rows), o...  80.4 us
    unnamed x13, local copies, waits for them, and re-layouts  10.3 us
    another operation x3, local copies, waits for them, and re-layouts, cell_cache(): jnp.stack([patch_counts, image_request, image_position])  2.29 us

profile of v3, /device:TPU:1, one launch (start us, length us, event | category | flops | bytes accessed | tf_op | source)
XLA Modules:
  0.0 97.1 jit_solution(2420813693526036693)
XLA Ops:
  0.0 0.7 broadcast_multiply_fusion
  0.7 0.1 mul.41
  0.8 0.8 copy.16
  1.6 0.8 copy.17
  2.3 0.8 copy.18
  3.1 0.7 reshape.48.vit_gain
  3.8 0.7 reshape.49.merge_gain
  4.5 0.1 broadcast_in_dim.7
  4.6 0.1 broadcast_in_dim.8.limits
  4.7 0.3 fusion
  5.0 0.1 pad_maximum_fusion
  5.1 0.0 copy-start
  5.1 0.0 copy-start.1
  5.1 0.0 copy-start.2
  5.1 0.0 copy-start.3
  5.1 0.0 copy-start.4
  5.1 0.0 copy-start.5
  5.1 10.3 %copy.19 = bf16[256,8,2,1024]{3,1,2,0:T(8,128)(2,1)} copy(bf16[256,8,2,1024]{3,2,1,0:T(2,128)(2,1)} %bitcast.9) | data formatting | bytes 16777216
  15.5 0.0 copy-done
  15.5 0.0 copy-done.1
  15.5 0.0 copy-done.2
  15.5 0.0 copy-done.3
  15.5 0.0 copy-done.4
  15.5 0.0 copy-done.5
  15.5 80.4 %shard_map.145 = bf16[128,2048]{1,0:T(8,128)(2,1)S(1)} custom-call(s32[3,4,2]{2,1,0:T(4,128)S(1)} %pad_add_fusion.tables, s32[4]{0:T(128)S(1)} %copy-done.5, bf16[64,320]{1,0:T(8,128)(2,1)S(1)} %copy-done.3, f32[1,1280]{1,0:T(1,128)S(1)} %reshape.48.vit_gain, f32[1,1280]{1,0:T(1,128)S(1)} %reshape.49.merge_gain, f32[1,2048]{1,0:T(1,128)S(1)} %bitcast.8, ...), custom_call_target="tpu_custom_call" | custom-call | flops 6000000000 | bytes 22000000 | tf_op jit(solution)/shard_map/pallas_call | solution.py:694
  95.9 1.2 %reshape.52 = bf16[128,2,1024]{2,1,0:T(2,128)(2,1)} reshape(bf16[128,2048]{1,0:T(8,128)(2,1)S(1)} %shard_map.145) | data formatting | bytes 1048576 | tf_op jit(solution)/shard_map/reshape | solution.py:765
  (3 shorter events, 0.0 us)
Async XLA Ops:
  5.1 10.4 %copy-start = (bf16[512,2048]{1,0:T(8,128)(2,1)S(1)}, bf16[512,2048]{1,0:T(8,128)(2,1)}, u32[]{:S(2)}) copy-start(bf16[512,2048]{1,0:T(8,128)(2,1)} %text_hbm.1) | copy-start | bytes 6291460
  5.1 10.4 %copy-start.1 = (bf16[320,3,320]{2,0,1:T(8,128)(2,1)S(1)}, bf16[320,3,320]{2,0,1:T(8,128)(2,1)}, u32[]{:S(2)}) copy-start(bf16[320,3,320]{2,0,1:T(8,128)(2,1)} %param.21) | copy-start | bytes 1843204
  5.1 10.4 %copy-start.2 = (bf16[320,320]{1,0:T(8,128)(2,1)S(1)}, bf16[320,320]{1,0:T(8,128)(2,1)}, u32[]{:S(2)}) copy-start(bf16[320,320]{1,0:T(8,128)(2,1)} %proj_hbm.1) | copy-start | bytes 614404
  5.1 10.4 %copy-start.3 = (bf16[64,320]{1,0:T(8,128)(2,1)S(1)}, bf16[64,320]{1,0:T(8,128)(2,1)}, u32[]{:S(2)}) copy-start(bf16[64,320]{1,0:T(8,128)(2,1)} %patches.1) | copy-start | bytes 122884
  5.1 10.4 %copy-start.4 = (f32[2048]{0:T(1024)S(1)}, f32[2048]{0:T(1024)}, u32[]{:S(2)}) copy-start(f32[2048]{0:T(1024)} %param.27) | copy-start | bytes 24580
  5.1 10.4 %copy-start.5 = (s32[4]{0:T(128)S(1)}, s32[4]{0:T(128)}, u32[]{:S(2)}) copy-start(s32[4]{0:T(128)} %lengths.1) | copy-start | bytes 52

commit v4 on v3

--- a/solution.py
+++ b/solution.py
@@ -232,8 +232,7 @@
     tables,
     lengths,
     patches,
-    vit_gain,
-    merge_gain,
+    norm_gains,
     rms_gain,
     cosines,
     sines,
@@ -262,6 +261,7 @@
     part_in,
     att_out,
     att_in,
+    branch_own,
     branch_out,
     branch_in,
     hid_out,
@@ -386,7 +386,7 @@
     for d in range(1, SIDE):
         receive(patch_all.at[other(t, SIDE - d)], 0, d)
 
-    def chunk_norm(values, gains):
+    def chunk_norm(values, k):
         total = jnp.sum(values[0], axis=1, keepdims=True)
         for v in values[1:]:
             total = total + jnp.sum(v, axis=1, keepdims=True)
@@ -397,11 +397,11 @@
             total = total + jnp.sum(v * v, axis=1, keepdims=True)
         inverse = lax.rsqrt(total / full + epsilon)
         return [
-            (v * inverse * gains[:, c * width : (c + 1) * width]).astype(jnp.bfloat16)
+            (v * inverse * norm_gains[k : k + 1, c * width : (c + 1) * width]).astype(jnp.bfloat16)
             for c, v in enumerate(centred)
         ]
 
-    normed = chunk_norm([patch_all[c].astype(jnp.float32) for c in range(SIDE)], vit_gain)
+    normed = chunk_norm([patch_all[c].astype(jnp.float32) for c in range(SIDE)], 0)
     for c in range(SIDE):
         norm_out[c] = normed[c]
     for d in range(1, SIDE):
@@ -485,18 +485,19 @@
     branch = f32_dot(att_in[...].reshape(SIDE * rows, width), proj_w[...])
     branch = branch.reshape(SIDE, SIDE, SLOTS, width)
     for c in range(SIDE):
-        branch_out[c] = branch[:, c].reshape(rows, width)
+        branch_own[c] = branch[:, c].reshape(rows, width)
+        branch_out[c] = branch_own[c].astype(jnp.bfloat16)
     for d in range(1, SIDE):
         c = other(t, d)
         send(remote(branch_out.at[c], branch_in.at[d - 1], 5, d, d, r, c))
-    total = branch_out[t]
+    total = branch_own[t]
     for d in range(SIDE):
         q = other(r, d)
         receive(res_in.at[q], 1, q, on_diagonal if d == 0 else None)
     residual = res_in[...].reshape(rows, width).astype(jnp.float32)
     for d in range(1, SIDE):
         receive(branch_in.at[d - 1], 5, d)
-        total = total + branch_in[d - 1]
+        total = total + branch_in[d - 1].astype(jnp.float32)
     hid_out[...] = (residual + total).astype(jnp.bfloat16)
     for d in range(SIDE):
         unless = on_diagonal if d == 0 else None
@@ -512,7 +513,7 @@
         q = other(r, d)
         receive(hid_in.at[q], 6, q, on_diagonal if d == 0 else None)
 
-    merged = chunk_norm([hid_in[c].astype(jnp.float32) for c in range(SIDE)], merge_gain)
+    merged = chunk_norm([hid_in[c].astype(jnp.float32) for c in range(SIDE)], 1)
     before = f32_dot(merged[0], fc1_w[0:width])
     for c in range(1, SIDE):
         before = before + f32_dot(merged[c], fc1_w[c * width : (c + 1) * width])
@@ -667,7 +668,8 @@
         ((rows, width), bf16),
         ((n, rows, width), bf16),
         ((n, rows, width), f32),
-        ((n - 1, rows, width), f32),
+        ((n, rows, width), bf16),
+        ((n - 1, rows, width), bf16),
         ((rows, width), bf16),
         ((n, rows, width), bf16),
         ((n, SLOTS, hidden_w), f32),
@@ -694,7 +696,7 @@
     return pl.pallas_call(
         functools.partial(cell_kernel, request_len, token_rows),
         out_shape=jax.ShapeDtypeStruct((share, kv_width), bf16),
-        in_specs=[smem] * 2 + [vmem] * 7 + [anywhere] * 6,
+        in_specs=[smem] * 2 + [vmem] * 6 + [anywhere] * 6,
         out_specs=vmem,
         scratch_shapes=scratch,
         compiler_params=pltpu.CompilerParams(
@@ -707,8 +709,7 @@
         jnp.stack([patch_counts, image_request, image_position]),
         request_lengths,
         patches,
-        vit_gain.reshape(1, n * width),
-        merge_gain.reshape(1, n * width),
+        jnp.stack([vit_gain, merge_gain]),
         rms_gain.reshape(1, share_w),
         jnp.concatenate([cosine, cosine], axis=1),
         jnp.concatenate([-sine, sine], axis=1),

time: 97.4 us -> 96.4 us (0.990)
  Pallas kernels: 80.4 us -> 79.4 us
    reshape x2 -> x0, local copies, waits for them, and re-layouts: 1.4 us -> none  [the longest x1 0.7 us: cell_cache(): vit_gain.reshape(1, n * width)]
    another operation x0 -> x2, local copies, waits for them, and re-layouts: none -> 1.4 us  [cell_cache(): jnp.stack([vit_gain, merge_gain])]
    pallas_call x1, Pallas kernels: 80.4 us -> 79.4 us  [cell_cache(): pl.pallas_call(functools.partial(cell_kernel, request_len, token_rows), o...]
where the time goes in v4:
time: 96.4 us; the launch traced here: 96.1 us
  Pallas kernels  79.4 us (82%)
  local copies, waits for them, and re-layouts  15.4 us (16%)
  other arithmetic  1.13 us (1%)
    pallas_call x1, Pallas kernels, cell_cache(): pl.pallas_call(functools.partial(cell_kernel, request_len, token_rows), o...  79.4 us
    unnamed x13, local copies, waits for them, and re-layouts  10.3 us
    another operation x3, local copies, waits for them, and re-layouts, cell_cache(): jnp.stack([patch_counts, image_request, image_position])  2.29 us

profile of v4, /device:TPU:1, one launch (start us, length us, event | category | flops | bytes accessed | tf_op | source)
XLA Modules:
  0.0 96.1 jit_solution(8425238330218234776)
XLA Ops:
  0.0 0.7 broadcast_multiply_fusion
  0.7 0.1 mul.41
  0.8 0.8 copy.16
  1.6 0.8 copy.17
  2.3 0.8 copy.18
  3.1 0.7 stack.25
  3.8 0.7 stack.26
  4.5 0.1 broadcast_in_dim.7
  4.6 0.1 broadcast_in_dim.8.limits
  4.7 0.3 fusion
  5.0 0.1 pad_maximum_fusion
  5.1 0.0 copy-start
  5.1 0.0 copy-start.1
  5.1 0.0 copy-start.2
  5.1 0.0 copy-start.3
  5.1 0.0 copy-start.4
  5.2 0.0 copy-start.5
  5.2 10.3 %copy.19 = bf16[256,8,2,1024]{3,1,2,0:T(8,128)(2,1)} copy(bf16[256,8,2,1024]{3,2,1,0:T(2,128)(2,1)} %bitcast.9) | data formatting | bytes 16777216
  15.5 0.0 copy-done
  15.5 0.0 copy-done.1
  15.5 0.0 copy-done.2
  15.5 0.0 copy-done.3
  15.5 0.0 copy-done.4
  15.5 0.0 copy-done.5
  15.5 79.4 %shard_map.145 = bf16[128,2048]{1,0:T(8,128)(2,1)S(1)} custom-call(s32[3,4,2]{2,1,0:T(4,128)S(1)} %pad_add_fusion.tables, s32[4]{0:T(128)S(1)} %copy-done.5, bf16[64,320]{1,0:T(8,128)(2,1)S(1)} %copy-done.3, f32[2,1280]{1,0:T(2,128)S(1)} %pad_maximum_fusion.2.norm_gains, f32[1,2048]{1,0:T(1,128)S(1)} %bitcast.8, f32[128,128]{1,0:T(8,128)S(1)} %get-tuple-element.8.cosines, ...), custom_call_target="tpu_custom_call" | custom-call | flops 6000000000 | bytes 22000000 | tf_op jit(solution)/shard_map/pallas_call | solution.py:696
  95.0 1.2 %reshape.44 = bf16[128,2,1024]{2,1,0:T(2,128)(2,1)} reshape(bf16[128,2048]{1,0:T(8,128)(2,1)S(1)} %shard_map.145) | data formatting | bytes 1048576 | tf_op jit(solution)/shard_map/reshape | solution.py:766
  (4 shorter events, 0.0 us)
Async XLA Ops:
  5.1 10.4 %copy-start = (bf16[512,2048]{1,0:T(8,128)(2,1)S(1)}, bf16[512,2048]{1,0:T(8,128)(2,1)}, u32[]{:S(2)}) copy-start(bf16[512,2048]{1,0:T(8,128)(2,1)} %text_hbm.1) | copy-start | bytes 6291460
  5.1 10.4 %copy-start.1 = (bf16[320,3,320]{2,0,1:T(8,128)(2,1)S(1)}, bf16[320,3,320]{2,0,1:T(8,128)(2,1)}, u32[]{:S(2)}) copy-start(bf16[320,3,320]{2,0,1:T(8,128)(2,1)} %param.21) | copy-start | bytes 1843204
  5.1 10.4 %copy-start.2 = (bf16[320,320]{1,0:T(8,128)(2,1)S(1)}, bf16[320,320]{1,0:T(8,128)(2,1)}, u32[]{:S(2)}) copy-start(bf16[320,320]{1,0:T(8,128)(2,1)} %proj_hbm.1) | copy-start | bytes 614404
  5.1 10.4 %copy-start.3 = (bf16[64,320]{1,0:T(8,128)(2,1)S(1)}, bf16[64,320]{1,0:T(8,128)(2,1)}, u32[]{:S(2)}) copy-start(bf16[64,320]{1,0:T(8,128)(2,1)} %patches.1) | copy-start | bytes 122884
  5.1 10.4 %copy-start.4 = (f32[2048]{0:T(1024)S(1)}, f32[2048]{0:T(1024)}, u32[]{:S(2)}) copy-start(f32[2048]{0:T(1024)} %param.27) | copy-start | bytes 24580
  5.2 10.4 %copy-start.5 = (s32[4]{0:T(128)S(1)}, s32[4]{0:T(128)}, u32[]{:S(2)}) copy-start(s32[4]{0:T(128)} %lengths.1) | copy-start | bytes 52
